TPU v7x, 32 devices: a whole 2x2x4 slice. The times are simulated.
32 devices in a mesh: section: 4 (over y, x), dp: 8 (over z, core).
Axes of the slice: x: 2, y: 2, z: 4, core: 2. Of those that a mesh axis runs over, the one named last changes fastest.
Arguments:
- tokens: bfloat16 [2048, 4096], P('dp'), may hold values from -6 to 6
- cotangent: bfloat16 [2048, 4096], P('dp'), may hold values from -30 to 30
- lengths: int32 [32], P('dp'), may hold values from 1 to 64
- seq_user: int32 [32], P('dp'), may hold values from 0 to 15, as said below
- norm_gains: float32 [4, 4096], P('section'), may hold values from 0.5 to 1.5
- weights: float32 [4, 4096, 2, 256], P('section', 'dp'), may hold values from -1 to 1
- first_moment: float32 [4, 4096, 2, 256], P('section', 'dp'), may hold values from -6 to 6
- second_moment: float32 [4, 4096, 2, 256], P('section', 'dp'), may hold values from 0.25 to 4
Outputs:
- new_first: float32 [4, 4096, 2, 256], P('section', 'dp')
- new_second: float32 [4, 4096, 2, 256], P('section', 'dp')
- step_dir: float32 [4, 4096, 2, 256], P('section', 'dp')
- user_ratio: float32 [16], P('dp')
Inputs may be any that keep to these rules, and one draw needn't show every extreme that they name: `seq_user`: the i-th block of 4 sequences carries only the user ids i * 2 to i * 2 + 1, each of them at least once.
All inputs are finite; a program needn't handle non-finite values.
Results may differ from a plain program's by a relative error of at most 0.0045.
Values may be sent and summed in bfloat16 or wider, within the bound.
A program may use at most 128 MiB of HBM per device.

v0:
```python
import jax
import jax.numpy as jnp
from jax import lax
from jax.sharding import PartitionSpec as P

SEQLEN = 64
USERS_DEV = 2


CLIP_BOUND = 70000.0
LOSS_SCALE = 1024.0
BETA_ONE = 0.9
BETA_TWO = 0.999
FIRST_FIX = 1.0 - 0.9**50
SECOND_FIX = 1.0 - 0.999**50
ADAM_EPS = 1e-08
NORM_EPS = 1e-05


def passed_along(value, axis, steps):
    count = lax.axis_size(axis)
    initial, last = (max(0, -steps), min(count, count - steps))
    return lax.ppermute(value, axis, [(source, source + steps) for source in range(initial, last)])


def section_forward(hidden, section_gain, down_cast, up_cast):
    widened = hidden.astype(jnp.float32)
    inverse = lax.rsqrt(jnp.mean(widened * widened, axis=-1, keepdims=True) + NORM_EPS)
    normed = (widened * inverse * section_gain).astype(jnp.bfloat16)
    inner_act = jnp.dot(normed, down_cast, preferred_element_type=jnp.float32)
    active = jax.nn.silu(inner_act).astype(jnp.bfloat16)
    branch = lax.dot_general(
        active, up_cast, (((1,), (1,)), ((), ())), preferred_element_type=jnp.float32
    )
    return ((widened + branch).astype(jnp.bfloat16), (widened, inverse, normed, inner_act, active))


def section_backward(grad_out, section_gain, down_cast, up_cast, kept_acts):
    widened, inverse, normed, inner_act, active = kept_acts
    grad_active = jnp.dot(grad_out, up_cast, preferred_element_type=jnp.float32)
    sigmoid_val = jax.nn.sigmoid(inner_act)
    grad_inner = (grad_active * sigmoid_val * (1.0 + inner_act * (1.0 - sigmoid_val))).astype(
        jnp.bfloat16
    )
    grad_normed = lax.dot_general(
        grad_inner, down_cast, (((1,), (1,)), ((), ())), preferred_element_type=jnp.float32
    )
    scaled = grad_normed * section_gain
    projected = jnp.mean(scaled * widened, axis=-1, keepdims=True)
    grad_in = (
        grad_out.astype(jnp.float32)
        + inverse * scaled
        - widened * inverse * inverse * inverse * projected
    )
    return (grad_in.astype(jnp.bfloat16), grad_inner)


def gram_of(values):
    return lax.dot_general(
        values, values, (((1,), (1,)), ((), ())), preferred_element_type=jnp.float32
    )


def user_squares(normed, grad_inner, active, grad_out, owners):
    joint = gram_of(normed) * gram_of(grad_inner) + gram_of(active) * gram_of(grad_out)
    spread = jnp.dot(joint, owners, precision=lax.Precision.HIGHEST)
    return jnp.sum(spread * owners, axis=0)


def keep_block(stored, produced, block_slot, blocks):
    usable = (block_slot >= 0) & (block_slot < blocks)
    clamped = jnp.clip(block_slot, 0, blocks - 1)
    if stored is None:
        stored = tuple(
            (jnp.zeros((blocks,) + element.shape, element.dtype) for element in produced)
        )
    updated = []
    for buffer, element in zip(stored, produced):
        before = lax.dynamic_index_in_dim(buffer, clamped, 0, keepdims=False)
        updated.append(
            lax.dynamic_update_index_in_dim(buffer, jnp.where(usable, element, before), clamped, 0)
        )
    return tuple(updated)


def active_width(stored):
    return stored[4].shape[-1]


def on_device(
    tokens, cotangent, lengths, seq_user, norm_gains, weights, first_moment, second_moment
):
    section_count = lax.axis_size("section")
    section_index = lax.axis_index("section")
    blocks = 4
    tok_rows = tokens.shape[0]
    model_width = tokens.shape[1]
    block_rows = tok_rows // blocks
    rounds = blocks + section_count - 1
    section_gain = norm_gains[0]
    packed = lax.all_gather(weights.astype(jnp.bfloat16), "dp", axis=1, tiled=True)
    down_cast = packed[0, :, 0, :]
    up_cast = packed[0, :, 1, :]
    inputs = tokens.reshape(blocks, block_rows, model_width)
    carried = jnp.zeros((block_rows, model_width), jnp.bfloat16)
    stored = None
    for step_no in range(rounds):
        incoming = jnp.where(section_index == 0, inputs[min(step_no, blocks - 1)], carried)
        result, kept_acts = section_forward(incoming, section_gain, down_cast, up_cast)
        stored = keep_block(stored, kept_acts, step_no - section_index, blocks)
        if step_no + 1 < rounds:
            carried = passed_along(result, "section", 1)
    positions = jnp.arange(tok_rows) % SEQLEN
    usable = positions < jnp.repeat(lengths, SEQLEN)
    local_user = seq_user - lax.axis_index("dp") * USERS_DEV
    token_user = jnp.repeat(local_user, SEQLEN)
    owners = ((token_user[:, None] == jnp.arange(USERS_DEV)[None, :]) & usable[:, None]).astype(
        jnp.float32
    )
    seed_rows = (cotangent * usable[:, None].astype(jnp.bfloat16)).reshape(
        blocks, block_rows, model_width
    )
    carried = jnp.zeros((block_rows, model_width), jnp.bfloat16)
    grad_store = None
    for step_no in range(rounds):
        block_slot = step_no - (section_count - 1 - section_index)
        clamped = jnp.clip(block_slot, 0, blocks - 1)
        incoming = jnp.where(
            section_index == section_count - 1, seed_rows[min(step_no, blocks - 1)], carried
        )
        kept_acts = tuple(
            (lax.dynamic_index_in_dim(buffer, clamped, 0, keepdims=False) for buffer in stored)
        )
        grad_in, grad_inner = section_backward(
            incoming, section_gain, down_cast, up_cast, kept_acts
        )
        grad_store = keep_block(grad_store, (incoming, grad_inner), block_slot, blocks)
        if step_no + 1 < rounds:
            carried = passed_along(grad_in, "section", -1)
    normed_all = stored[2].reshape(tok_rows, model_width)
    active_all = stored[4].reshape(tok_rows, active_width(stored))
    grad_out_all = grad_store[0].reshape(tok_rows, model_width)
    grad_inner_all = grad_store[1].reshape(tok_rows, active_width(stored))
    local_squares = user_squares(normed_all, grad_inner_all, active_all, grad_out_all, owners)
    squares = lax.psum(local_squares, "section")
    user_norm = jnp.sqrt(squares)
    factors = LOSS_SCALE / jnp.maximum(user_norm, CLIP_BOUND)
    token_factor = jnp.dot(owners, factors, precision=lax.Precision.HIGHEST)
    weighted_inner = (grad_inner_all.astype(jnp.float32) * token_factor[:, None]).astype(
        jnp.bfloat16
    )
    weighted_out = (grad_out_all.astype(jnp.float32) * token_factor[:, None]).astype(jnp.bfloat16)
    down_term = lax.dot_general(
        normed_all, weighted_inner, (((0,), (0,)), ((), ())), preferred_element_type=jnp.float32
    )
    up_term = lax.dot_general(
        weighted_out, active_all, (((0,), (0,)), ((), ())), preferred_element_type=jnp.float32
    )
    gradient = lax.psum_scatter(
        jnp.stack([down_term, up_term], axis=1).astype(jnp.bfloat16),
        "dp",
        scatter_dimension=0,
        tiled=True,
    ).astype(jnp.float32)
    moment_one = BETA_ONE * first_moment[0] + (1.0 - BETA_ONE) * gradient
    moment_two = BETA_TWO * second_moment[0] + (1.0 - BETA_TWO) * gradient * gradient
    direction = moment_one / FIRST_FIX / (jnp.sqrt(moment_two / SECOND_FIX) + ADAM_EPS)
    return (moment_one[None], moment_two[None], direction[None], user_norm / CLIP_BOUND)


def solution(mesh):
    return jax.shard_map(
        on_device,
        mesh=mesh,
        in_specs=(
            P("dp", None),
            P("dp", None),
            P("dp"),
            P("dp"),
            P("section", None),
            P("section", "dp", None, None),
            P("section", "dp", None, None),
            P("section", "dp", None, None),
        ),
        out_specs=(
            P("section", "dp", None, None),
            P("section", "dp", None, None),
            P("section", "dp", None, None),
            P("dp"),
        ),
        check_vma=False,
    )
```

profile of v0, /device:TPU:0, one launch (start us, length us, event | category | flops | bytes accessed | tf_op | source)
XLA Modules:
  0.0 347.7 jit_solution(9032892746187331166)
XLA Ops:
  7.2 2.2 copy.38
  15.0 2.5 broadcast_in_dim.191
  19.9 40.2 %all-gather.2.cloned.1.call-done = bf16[1,4096,2,256]{3,1,2,0:T(8,128)(2,1)} async-done(((bf16[1,512,2,256]{3,1,2,0:T(8,128)(2,1)}), bf16[1,4096,2,256]{3,1,2,0:T(8,128)(2,1)}) %all-gather.2.cloned.1.call-update) | async-done | bytes 4194320 | tf_op jit(solution)/shard_map/all_gather | solution.py:101
  60.1 2.4 bitcast_dynamic-update-slice_fusion.27
  63.1 2.6 fusion.4
  65.7 4.2 %collective-permute-start = (bf16[64,4096]{1,0:T(8,128)(2,1)}, bf16[64,4096]{1,0:T(8,128)(2,1)}, u32[]{:S(2)}, u32[]{:S(2)}) collective-permute-start(bf16[64,4096]{1,0:T(8,128)(2,1)} %fusion.4), channel_id=1, source_target_pairs={{0,8},{8,16},{16,24},{1,9},{9,17},{17,25},{2,10},{10,18},{18,26},{... | collective-permute-start | bytes 1572872 | tf_op jit(solution)/shard_map/ppermute | solution.py:23
  70.1 10.8 %collective-permute-done = bf16[64,4096]{1,0:T(8,128)(2,1)} collective-permute-done((bf16[64,4096]{1,0:T(8,128)(2,1)}, bf16[64,4096]{1,0:T(8,128)(2,1)}, u32[]{:S(2)}, u32[]{:S(2)}) %collective-permute-start) | collective-permute-done | bytes 524320 | tf_op jit(solution)/shard_map/ppermute | solution.py:23
  80.9 2.2 fusion.46
  84.7 4.7 %collective-permute-start.1 = (bf16[64,4096]{1,0:T(8,128)(2,1)S(1)}, bf16[64,4096]{1,0:T(8,128)(2,1)S(1)}, u32[]{:S(2)}, u32[]{:S(2)}) collective-permute-start(bf16[64,4096]{1,0:T(8,128)(2,1)S(1)} %fusion.5), channel_id=1, source_target_pairs={{0,8},{8,16},{16,24},{1,9},{9,17},{17,25},{2,10},{10,18},{18,26},{... | collective-permute-start | bytes 1572872 | tf_op jit(solution)/shard_map/ppermute | solution.py:23
  91.4 8.7 %collective-permute-done.1 = bf16[64,4096]{1,0:T(8,128)(2,1)S(1)} collective-permute-done((bf16[64,4096]{1,0:T(8,128)(2,1)S(1)}, bf16[64,4096]{1,0:T(8,128)(2,1)S(1)}, u32[]{:S(2)}, u32[]{:S(2)}) %collective-permute-start.1) | collective-permute-done | bytes 524320 | tf_op jit(solution)/shard_map/ppermute | solution.py:23
  102.8 4.4 %collective-permute-start.2 = (bf16[64,4096]{1,0:T(8,128)(2,1)S(1)}, bf16[64,4096]{1,0:T(8,128)(2,1)S(1)}, u32[]{:S(2)}, u32[]{:S(2)}) collective-permute-start(bf16[64,4096]{1,0:T(8,128)(2,1)S(1)} %fusion.6), channel_id=1, source_target_pairs={{0,8},{8,16},{16,24},{1,9},{9,17},{17,25},{2,10},{10,18},{18,26},{... | collective-permute-start | bytes 1572872 | tf_op jit(solution)/shard_map/ppermute | solution.py:23
  109.0 8.0 %collective-permute-done.2 = bf16[64,4096]{1,0:T(8,128)(2,1)S(1)} collective-permute-done((bf16[64,4096]{1,0:T(8,128)(2,1)S(1)}, bf16[64,4096]{1,0:T(8,128)(2,1)S(1)}, u32[]{:S(2)}, u32[]{:S(2)}) %collective-permute-start.2) | collective-permute-done | bytes 524320 | tf_op jit(solution)/shard_map/ppermute | solution.py:23
  119.7 5.1 %collective-permute-start.3 = (bf16[64,4096]{1,0:T(8,128)(2,1)S(1)}, bf16[64,4096]{1,0:T(8,128)(2,1)S(1)}, u32[]{:S(2)}, u32[]{:S(2)}) collective-permute-start(bf16[64,4096]{1,0:T(8,128)(2,1)S(1)} %fusion.7), channel_id=1, source_target_pairs={{0,8},{8,16},{16,24},{1,9},{9,17},{17,25},{2,10},{10,18},{18,26},{... | collective-permute-start | bytes 1572872 | tf_op jit(solution)/shard_map/ppermute | solution.py:23
  126.6 7.1 %collective-permute-done.3 = bf16[64,4096]{1,0:T(8,128)(2,1)S(1)} collective-permute-done((bf16[64,4096]{1,0:T(8,128)(2,1)S(1)}, bf16[64,4096]{1,0:T(8,128)(2,1)S(1)}, u32[]{:S(2)}, u32[]{:S(2)}) %collective-permute-start.3) | collective-permute-done | bytes 524320 | tf_op jit(solution)/shard_map/ppermute | solution.py:23
  136.5 5.3 %collective-permute-start.4 = (bf16[64,4096]{1,0:T(8,128)(2,1)S(1)}, bf16[64,4096]{1,0:T(8,128)(2,1)S(1)}, u32[]{:S(2)}, u32[]{:S(2)}) collective-permute-start(bf16[64,4096]{1,0:T(8,128)(2,1)S(1)} %fusion.8), channel_id=1, source_target_pairs={{0,8},{8,16},{16,24},{1,9},{9,17},{17,25},{2,10},{10,18},{18,26},{... | collective-permute-start | bytes 1572872 | tf_op jit(solution)/shard_map/ppermute | solution.py:23
  143.6 6.2 %collective-permute-done.4 = bf16[64,4096]{1,0:T(8,128)(2,1)S(1)} collective-permute-done((bf16[64,4096]{1,0:T(8,128)(2,1)S(1)}, bf16[64,4096]{1,0:T(8,128)(2,1)S(1)}, u32[]{:S(2)}, u32[]{:S(2)}) %collective-permute-start.4) | collective-permute-done | bytes 524320 | tf_op jit(solution)/shard_map/ppermute | solution.py:23
  152.5 5.4 %collective-permute-start.5 = (bf16[64,4096]{1,0:T(8,128)(2,1)S(1)}, bf16[64,4096]{1,0:T(8,128)(2,1)S(1)}, u32[]{:S(2)}, u32[]{:S(2)}) collective-permute-start(bf16[64,4096]{1,0:T(8,128)(2,1)S(1)} %fusion.9), channel_id=1, source_target_pairs={{0,8},{8,16},{16,24},{1,9},{9,17},{17,25},{2,10},{10,18},{18,26},{... | collective-permute-start | bytes 1572872 | tf_op jit(solution)/shard_map/ppermute | solution.py:23
  159.7 5.1 %collective-permute-done.5 = bf16[64,4096]{1,0:T(8,128)(2,1)S(1)} collective-permute-done((bf16[64,4096]{1,0:T(8,128)(2,1)S(1)}, bf16[64,4096]{1,0:T(8,128)(2,1)S(1)}, u32[]{:S(2)}, u32[]{:S(2)}) %collective-permute-start.5) | collective-permute-done | bytes 524320 | tf_op jit(solution)/shard_map/ppermute | solution.py:23
  168.3 2.1 fusion.102
  175.0 9.5 %collective-permute-done.6 = bf16[64,4096]{1,0:T(8,128)(2,1)S(1)} collective-permute-done((bf16[64,4096]{1,0:T(8,128)(2,1)S(1)}, bf16[64,4096]{1,0:T(8,128)(2,1)S(1)}, u32[]{:S(2)}, u32[]{:S(2)}) %collective-permute-start.6) | collective-permute-done | bytes 524320 | tf_op jit(solution)/shard_map/ppermute | solution.py:23
  185.3 2.1 fusion.96
  190.4 11.1 %collective-permute-done.7 = bf16[64,4096]{1,0:T(8,128)(2,1)S(1)} collective-permute-done((bf16[64,4096]{1,0:T(8,128)(2,1)S(1)}, bf16[64,4096]{1,0:T(8,128)(2,1)S(1)}, u32[]{:S(2)}, u32[]{:S(2)}) %collective-permute-start.7) | collective-permute-done | bytes 524320 | tf_op jit(solution)/shard_map/ppermute | solution.py:23
  202.2 2.1 fusion.90
  207.3 10.6 %collective-permute-done.8 = bf16[64,4096]{1,0:T(8,128)(2,1)S(1)} collective-permute-done((bf16[64,4096]{1,0:T(8,128)(2,1)S(1)}, bf16[64,4096]{1,0:T(8,128)(2,1)S(1)}, u32[]{:S(2)}, u32[]{:S(2)}) %collective-permute-start.8) | collective-permute-done | bytes 524320 | tf_op jit(solution)/shard_map/ppermute | solution.py:23
  218.7 2.1 fusion.84
  223.8 10.6 %collective-permute-done.9 = bf16[64,4096]{1,0:T(8,128)(2,1)S(1)} collective-permute-done((bf16[64,4096]{1,0:T(8,128)(2,1)S(1)}, bf16[64,4096]{1,0:T(8,128)(2,1)S(1)}, u32[]{:S(2)}, u32[]{:S(2)}) %collective-permute-start.9) | collective-permute-done | bytes 524320 | tf_op jit(solution)/shard_map/ppermute | solution.py:23
  235.1 2.1 fusion.78
  240.2 11.0 %collective-permute-done.10 = bf16[64,4096]{1,0:T(8,128)(2,1)S(1)} collective-permute-done((bf16[64,4096]{1,0:T(8,128)(2,1)S(1)}, bf16[64,4096]{1,0:T(8,128)(2,1)S(1)}, u32[]{:S(2)}, u32[]{:S(2)}) %collective-permute-start.10) | collective-permute-done | bytes 524320 | tf_op jit(solution)/shard_map/ppermute | solution.py:23
  257.4 10.8 %collective-permute-done.11 = bf16[64,4096]{1,0:T(8,128)(2,1)S(1)} collective-permute-done((bf16[64,4096]{1,0:T(8,128)(2,1)S(1)}, bf16[64,4096]{1,0:T(8,128)(2,1)S(1)}, u32[]{:S(2)}, u32[]{:S(2)}) %collective-permute-start.11) | collective-permute-done | bytes 524320 | tf_op jit(solution)/shard_map/ppermute | solution.py:23
  270.4 10.4 %psum.7 = f32[2]{0:T(128)S(1)} all-reduce(f32[2]{0:T(128)S(1)} %fusion.29), channel_id=1, replica_groups=mesh['section'=4,'dp'=8] {'section'}, use_global_device_ids=true, to_apply=%region_14.15 | all-reduce | flops 2 | bytes 16 | tf_op jit(solution)/shard_map/psum | solution.py:145
  283.4 2.3 pad_maximum_fusion
  286.3 47.5 %reduce-scatter.2.cloned.1.call-done = bf16[512,2,256]{2,0,1:T(8,128)(2,1)} async-done(((bf16[4096,2,256]{2,0,1:T(8,128)(2,1)}), bf16[512,2,256]{2,0,1:T(8,128)(2,1)}) %reduce-scatter.2.cloned.1.call-update) | async-done | bytes 524304 | tf_op jit(solution)/shard_map/reduce_scatter | solution.py:159
  (189 shorter events, 71.1 us)
Async XLA Ops:
  7.2 2.4 copy-start.16
  7.2 3.9 %copy-start.12 = (bf16[256,4096]{1,0:T(8,128)(2,1)S(1)}, bf16[256,4096]{1,0:T(8,128)(2,1)}, u32[]{:S(2)}) copy-start(bf16[256,4096]{1,0:T(8,128)(2,1)} %param.9) | copy-start | bytes 6291460
  7.2 52.9 %all-gather.2.cloned.1.call-start = ((), (), s32[]{:S(2)}) async-start(), calls=%async_computation.1 | async-start | bytes 4718592 | tf_op jit(solution)/shard_map/all_gather | solution.py:101
  9.5 324.3 %reduce-scatter.2.cloned.1.call-start = ((), (), s32[]{:S(2)}) async-start(), calls=%async_computation.2 | async-start | bytes 4718592 | tf_op jit(solution)/shard_map/reduce_scatter | solution.py:159
  11.3 1.6 copy-start.6
  11.5 2.3 copy-start.8
  11.5 2.3 copy-start.10
  14.0 3.4 copy-start.2
  60.1 3.0 copy-start
  62.6 7.3 %copy-start.17 = (s32[4]{0:T(128)S(1)}, s32[4]{0:T(128)}, u32[]{:S(2)}) copy-start(s32[4]{0:T(128)} %param.11) | copy-start | bytes 52
  65.7 15.3 %collective-permute-start = (bf16[64,4096]{1,0:T(8,128)(2,1)}, bf16[64,4096]{1,0:T(8,128)(2,1)}, u32[]{:S(2)}, u32[]{:S(2)}) collective-permute-start(bf16[64,4096]{1,0:T(8,128)(2,1)} %fusion.4), channel_id=1, source_target_pairs={{0,8},{8,16},{16,24},{1,9},{9,17},{17,25},{2,10},{10,18},{18,26},{... | collective-permute-start | bytes 1572872 | tf_op jit(solution)/shard_map/ppermute | solution.py:23
  70.1 13.2 %copy-start.1 = (bf16[1,4096,2,256]{3,1,2,0:T(8,128)(2,1)S(1)}, bf16[1,4096,2,256]{3,1,2,0:T(8,128)(2,1)}, u32[]{:S(2)}) copy-start(bf16[1,4096,2,256]{3,1,2,0:T(8,128)(2,1)} %all-gather.2.cloned.1.call-done) | copy-start | bytes 12582916
  83.9 5.5 %copy-start.3 = (bf16[4,64,4096]{2,1,0:T(8,128)(2,1)S(1)}, bf16[4,64,4096]{2,1,0:T(8,128)(2,1)}, u32[]{:S(2)}) copy-start(bf16[4,64,4096]{2,1,0:T(8,128)(2,1)} %copy-done.2) | copy-start | bytes 6291460
  83.9 5.5 %copy-start.11 = (bf16[1,64,4096]{2,1,0:T(8,128)(2,1)S(1)}, bf16[1,64,4096]{2,1,0:T(8,128)(2,1)}, u32[]{:S(2)}) copy-start(bf16[1,64,4096]{2,1,0:T(8,128)(2,1)} %constant_dynamic-slice_fusion.47) | copy-start | bytes 1572868
  84.7 15.4 %collective-permute-start.1 = (bf16[64,4096]{1,0:T(8,128)(2,1)S(1)}, bf16[64,4096]{1,0:T(8,128)(2,1)S(1)}, u32[]{:S(2)}, u32[]{:S(2)}) collective-permute-start(bf16[64,4096]{1,0:T(8,128)(2,1)S(1)} %fusion.5), channel_id=1, source_target_pairs={{0,8},{8,16},{16,24},{1,9},{9,17},{17,25},{2,10},{10,18},{18,26},{... | collective-permute-start | bytes 1572872 | tf_op jit(solution)/shard_map/ppermute | solution.py:23
  89.4 10.7 %copy-start.9 = (bf16[256,4096]{1,0:T(8,128)(2,1)S(1)}, bf16[256,4096]{1,0:T(8,128)(2,1)}, u32[]{:S(2)}) copy-start(bf16[256,4096]{1,0:T(8,128)(2,1)} %param.8) | copy-start | bytes 6291460
  102.8 14.2 %collective-permute-start.2 = (bf16[64,4096]{1,0:T(8,128)(2,1)S(1)}, bf16[64,4096]{1,0:T(8,128)(2,1)S(1)}, u32[]{:S(2)}, u32[]{:S(2)}) collective-permute-start(bf16[64,4096]{1,0:T(8,128)(2,1)S(1)} %fusion.6), channel_id=1, source_target_pairs={{0,8},{8,16},{16,24},{1,9},{9,17},{17,25},{2,10},{10,18},{18,26},{... | collective-permute-start | bytes 1572872 | tf_op jit(solution)/shard_map/ppermute | solution.py:23
  119.7 14.0 %collective-permute-start.3 = (bf16[64,4096]{1,0:T(8,128)(2,1)S(1)}, bf16[64,4096]{1,0:T(8,128)(2,1)S(1)}, u32[]{:S(2)}, u32[]{:S(2)}) collective-permute-start(bf16[64,4096]{1,0:T(8,128)(2,1)S(1)} %fusion.7), channel_id=1, source_target_pairs={{0,8},{8,16},{16,24},{1,9},{9,17},{17,25},{2,10},{10,18},{18,26},{... | collective-permute-start | bytes 1572872 | tf_op jit(solution)/shard_map/ppermute | solution.py:23
  136.5 13.3 %collective-permute-start.4 = (bf16[64,4096]{1,0:T(8,128)(2,1)S(1)}, bf16[64,4096]{1,0:T(8,128)(2,1)S(1)}, u32[]{:S(2)}, u32[]{:S(2)}) collective-permute-start(bf16[64,4096]{1,0:T(8,128)(2,1)S(1)} %fusion.8), channel_id=1, source_target_pairs={{0,8},{8,16},{16,24},{1,9},{9,17},{17,25},{2,10},{10,18},{18,26},{... | collective-permute-start | bytes 1572872 | tf_op jit(solution)/shard_map/ppermute | solution.py:23
  152.5 12.3 %collective-permute-start.5 = (bf16[64,4096]{1,0:T(8,128)(2,1)S(1)}, bf16[64,4096]{1,0:T(8,128)(2,1)S(1)}, u32[]{:S(2)}, u32[]{:S(2)}) collective-permute-start(bf16[64,4096]{1,0:T(8,128)(2,1)S(1)} %fusion.9), channel_id=1, source_target_pairs={{0,8},{8,16},{16,24},{1,9},{9,17},{17,25},{2,10},{10,18},{18,26},{... | collective-permute-start | bytes 1572872 | tf_op jit(solution)/shard_map/ppermute | solution.py:23
  166.2 1.6 copy-start.7
  172.1 12.4 %collective-permute-start.6 = (bf16[64,4096]{1,0:T(8,128)(2,1)S(1)}, bf16[64,4096]{1,0:T(8,128)(2,1)S(1)}, u32[]{:S(2)}, u32[]{:S(2)}) collective-permute-start(bf16[64,4096]{1,0:T(8,128)(2,1)S(1)} %fusion.101), channel_id=1, source_target_pairs={{8,0},{16,8},{24,16},{9,1},{17,9},{25,17},{10,2},{18,10},{26,18},{... | collective-permute-start | bytes 1572872 | tf_op jit(solution)/shard_map/ppermute | solution.py:23
  173.7 1.3 copy-start.4
  173.7 10.8 %copy-start.13 = (bf16[1,64,4096]{2,1,0:T(8,128)(2,1)S(1)}, bf16[1,64,4096]{2,1,0:T(8,128)(2,1)}, u32[]{:S(2)}) copy-start(bf16[1,64,4096]{2,1,0:T(8,128)(2,1)} %constant_dynamic-slice_fusion.5) | copy-start | bytes 1572868
  189.0 12.4 %collective-permute-start.7 = (bf16[64,4096]{1,0:T(8,128)(2,1)S(1)}, bf16[64,4096]{1,0:T(8,128)(2,1)S(1)}, u32[]{:S(2)}, u32[]{:S(2)}) collective-permute-start(bf16[64,4096]{1,0:T(8,128)(2,1)S(1)} %fusion.95), channel_id=1, source_target_pairs={{8,0},{16,8},{24,16},{9,1},{17,9},{25,17},{10,2},{18,10},{26,18},{... | collective-permute-start | bytes 1572872 | tf_op jit(solution)/shard_map/ppermute | solution.py:23
  205.9 12.0 %collective-permute-start.8 = (bf16[64,4096]{1,0:T(8,128)(2,1)S(1)}, bf16[64,4096]{1,0:T(8,128)(2,1)S(1)}, u32[]{:S(2)}, u32[]{:S(2)}) collective-permute-start(bf16[64,4096]{1,0:T(8,128)(2,1)S(1)} %fusion.89), channel_id=1, source_target_pairs={{8,0},{16,8},{24,16},{9,1},{17,9},{25,17},{10,2},{18,10},{26,18},{... | collective-permute-start | bytes 1572872 | tf_op jit(solution)/shard_map/ppermute | solution.py:23
  222.4 12.0 %collective-permute-start.9 = (bf16[64,4096]{1,0:T(8,128)(2,1)S(1)}, bf16[64,4096]{1,0:T(8,128)(2,1)S(1)}, u32[]{:S(2)}, u32[]{:S(2)}) collective-permute-start(bf16[64,4096]{1,0:T(8,128)(2,1)S(1)} %fusion.83), channel_id=1, source_target_pairs={{8,0},{16,8},{24,16},{9,1},{17,9},{25,17},{10,2},{18,10},{26,18},{... | collective-permute-start | bytes 1572872 | tf_op jit(solution)/shard_map/ppermute | solution.py:23
  238.9 12.4 %collective-permute-start.10 = (bf16[64,4096]{1,0:T(8,128)(2,1)S(1)}, bf16[64,4096]{1,0:T(8,128)(2,1)S(1)}, u32[]{:S(2)}, u32[]{:S(2)}) collective-permute-start(bf16[64,4096]{1,0:T(8,128)(2,1)S(1)} %fusion.77), channel_id=1, source_target_pairs={{8,0},{16,8},{24,16},{9,1},{17,9},{25,17},{10,2},{18,10},{26,18},{... | collective-permute-start | bytes 1572872 | tf_op jit(solution)/shard_map/ppermute | solution.py:23
  255.8 12.4 %collective-permute-start.11 = (bf16[64,4096]{1,0:T(8,128)(2,1)S(1)}, bf16[64,4096]{1,0:T(8,128)(2,1)S(1)}, u32[]{:S(2)}, u32[]{:S(2)}) collective-permute-start(bf16[64,4096]{1,0:T(8,128)(2,1)S(1)} %fusion.71), channel_id=1, source_target_pairs={{8,0},{16,8},{24,16},{9,1},{17,9},{25,17},{10,2},{18,10},{26,18},{... | collective-permute-start | bytes 1572872 | tf_op jit(solution)/shard_map/ppermute | solution.py:23
  281.0 1.6 copy-start.5
  285.8 48.0 %copy-start.14 = (f32[1,512,2,256]{3,2,1,0:T(2,128)S(1)}, f32[1,512,2,256]{3,2,1,0:T(2,128)}, u32[]{:S(2)}) copy-start(f32[1,512,2,256]{3,2,1,0:T(2,128)} %param.14) | copy-start | bytes 3145732
  285.8 48.0 %copy-start.15 = (f32[1,512,2,256]{3,2,1,0:T(2,128)S(1)}, f32[1,512,2,256]{3,2,1,0:T(2,128)}, u32[]{:S(2)}) copy-start(f32[1,512,2,256]{3,2,1,0:T(2,128)} %param.15) | copy-start | bytes 3145732
Sparse Core Ops, SparseCore 0:
  10.2 49.8 all-gather.1
  285.9 47.8 reduce-scatter.1
where the time goes:
time: 349 us; the launch traced here: 348 us
  waiting for transfers between devices  197 us (56%)
  starting transfers between devices  37.2 us (11%)
  matrix products  32.3 us (9%)
  other arithmetic  30.4 us (9%)
  local copies, waits for them, and re-layouts  25.1 us (7%)
  between operations  15.1 us (4%)
  blocking collectives  10.4 us (3%)
    ppermute x12, waiting for transfers between devices, passed_along(): lax.ppermute(value, axis, [(source, source + steps) for source in range(i...  109 us
    reduce_scatter x1, waiting for transfers between devices, on_device(): lax.psum_scatter(jnp.stack([down_term, up_term], axis=1).astype(jnp.bfloa...  47.5 us
    all_gather x1, waiting for transfers between devices, on_device(): lax.all_gather(weights.astype(jnp.bfloat16), 'dp', axis=1, tiled=True)  40.2 us
    ppermute x12, starting transfers between devices, passed_along(): lax.ppermute(value, axis, [(source, source + steps) for source in range(i...  37.2 us
    dynamic_update_slice x35, other arithmetic, keep_block(): lax.dynamic_update_index_in_dim(buffer, jnp.where(usable, element, before...  13.4 us
    dot_general x6, matrix products, section_backward(): lax.dot_general(grad_inner, down_cast, (((1,), (1,)), ((), ())), preferre...  12.6 us
    unnamed x40, local copies, waits for them, and re-layouts  11.3 us
    dynamic_slice x36, local copies, waits for them, and re-layouts, keep_block(): before = lax.dynamic_index_in_dim(buffer, clamped, 0, keepdims=False)  10.4 us
  transfers between devices with their start and end apart: 14, of which 14 were waited for; matrix products, arithmetic and copies ran while one was open for 6% of the time, Pallas kernels for 0%

commit v1 on v0

v1 whole, which is shorter than its diff:
```python
import jax
import jax.numpy as jnp
from jax import lax
from jax.sharding import PartitionSpec as P

SEQLEN = 64
USERS_DEV = 2


CLIP_BOUND = 70000.0
LOSS_SCALE = 1024.0
BETA_ONE = 0.9
BETA_TWO = 0.999
FIRST_FIX = 1.0 - 0.9**50
SECOND_FIX = 1.0 - 0.999**50
ADAM_EPS = 1e-08
NORM_EPS = 1e-05


def dot_nt(left, right):
    return lax.dot_general(
        left, right, (((1,), (1,)), ((), ())), preferred_element_type=jnp.float32
    )


def dot_tn(left, right):
    return lax.dot_general(
        left, right, (((0,), (0,)), ((), ())), preferred_element_type=jnp.float32
    )


def on_device(
    tokens, cotangent, lengths, seq_user, norm_gains, weights, first_moment, second_moment
):
    sections = lax.axis_size("section")
    quarter = lax.axis_index("section")
    shards = lax.axis_size("dp")
    tok_rows, model_width = tokens.shape
    own_rows, _, width = weights.shape[1:]
    part = own_rows // sections
    held = shards * part

    def own_features(values):
        split = values.reshape(tok_rows, shards, sections, part)
        return lax.dynamic_index_in_dim(split, quarter, 2, keepdims=False).reshape(tok_rows, held)

    low = weights[0].astype(jnp.bfloat16).reshape(sections, part, 2, width)
    low = lax.all_to_all(low.transpose(0, 2, 1, 3), "section", 0, 0, tiled=True)
    low = lax.all_gather(low, "dp", axis=2, tiled=True)
    gains = norm_gains[0].reshape(shards, sections, part).transpose(1, 0, 2)
    gains = lax.all_to_all(gains.reshape(sections, held), "section", 0, 0, tiled=True)

    positions = jnp.arange(tok_rows) % SEQLEN
    usable = positions < jnp.repeat(lengths, SEQLEN)
    local_user = seq_user - lax.axis_index("dp") * USERS_DEV
    token_user = jnp.repeat(local_user, SEQLEN)
    owners = ((token_user[:, None] == jnp.arange(USERS_DEV)[None, :]) & usable[:, None]).astype(
        jnp.float32
    )

    hidden = own_features(tokens)
    kept = []
    for s in range(sections):
        down, up = low[s, 0], low[s, 1]
        widened = hidden.astype(jnp.float32)
        scaled = (widened * gains[s]).astype(jnp.bfloat16)
        product = jnp.dot(scaled, down, preferred_element_type=jnp.float32)
        total, product = lax.psum(
            (jnp.sum(widened * widened, axis=-1, keepdims=True), product), "section"
        )
        inverse = lax.rsqrt(total / model_width + NORM_EPS)
        inner = product * inverse
        active = jax.nn.silu(inner).astype(jnp.bfloat16)
        kept.append((widened, scaled, inverse, inner, active))
        hidden = (widened + dot_nt(active, up)).astype(jnp.bfloat16)

    grad_out = own_features(cotangent) * usable[:, None].astype(jnp.bfloat16)
    records = [None] * sections
    joint = jnp.zeros((tok_rows, tok_rows), jnp.float32)
    for s in reversed(range(sections)):
        down, up = low[s, 0], low[s, 1]
        widened, scaled, inverse, inner, active = kept[s]
        grad_active = lax.psum(
            jnp.dot(grad_out, up, preferred_element_type=jnp.float32), "section"
        )
        sigmoid_val = jax.nn.sigmoid(inner)
        grad_inner = grad_active * sigmoid_val * (1.0 + inner * (1.0 - sigmoid_val))
        grad_scaled = (grad_inner * inverse).astype(jnp.bfloat16)
        pull = jnp.sum(grad_inner * inner, axis=-1, keepdims=True) * (
            inverse * inverse / model_width
        )
        records[s] = (scaled, grad_scaled, grad_out, active)
        joint = joint + dot_nt(scaled, scaled) * dot_nt(grad_scaled, grad_scaled)
        joint = joint + dot_nt(active, active) * dot_nt(grad_out, grad_out)
        if s > 0:
            grad_out = (
                grad_out.astype(jnp.float32)
                + gains[s] * dot_nt(grad_scaled, down)
                - widened * pull
            ).astype(jnp.bfloat16)

    spread = jnp.dot(joint, owners, precision=lax.Precision.HIGHEST)
    squares = lax.psum(jnp.sum(spread * owners, axis=0), "section")
    user_norm = jnp.sqrt(squares)
    factors = LOSS_SCALE / jnp.maximum(user_norm, CLIP_BOUND)
    token_factor = jnp.dot(owners, factors, precision=lax.Precision.HIGHEST)[:, None]
    terms = []
    for scaled, grad_scaled, grad_out, active in records:
        weighted_inner = (grad_scaled.astype(jnp.float32) * token_factor).astype(jnp.bfloat16)
        weighted_out = (grad_out.astype(jnp.float32) * token_factor).astype(jnp.bfloat16)
        terms.append(
            jnp.stack([dot_tn(scaled, weighted_inner), dot_tn(weighted_out, active)], axis=0)
        )
    gradient = jnp.stack(terms, axis=0).astype(jnp.bfloat16)
    gradient = lax.psum_scatter(gradient, "dp", scatter_dimension=2, tiled=True)
    gradient = lax.all_to_all(gradient, "section", 0, 0, tiled=True)
    gradient = gradient.transpose(0, 2, 1, 3).reshape(own_rows, 2, width).astype(jnp.float32)
    moment_one = BETA_ONE * first_moment[0] + (1.0 - BETA_ONE) * gradient
    moment_two = BETA_TWO * second_moment[0] + (1.0 - BETA_TWO) * gradient * gradient
    direction = moment_one / FIRST_FIX / (jnp.sqrt(moment_two / SECOND_FIX) + ADAM_EPS)
    return (moment_one[None], moment_two[None], direction[None], user_norm / CLIP_BOUND)


def solution(mesh):
    return jax.shard_map(
        on_device,
        mesh=mesh,
        in_specs=(
            P("dp", None),
            P("dp", None),
            P("dp"),
            P("dp"),
            P("section", None),
            P("section", "dp", None, None),
            P("section", "dp", None, None),
            P("section", "dp", None, None),
        ),
        out_specs=(
            P("section", "dp", None, None),
            P("section", "dp", None, None),
            P("section", "dp", None, None),
            P("dp"),
        ),
        check_vma=False,
    )
```

time: 349 us -> 503 us (1.44)
  waiting for transfers between devices: 197 us -> 334 us
  blocking collectives: 10.4 us -> 59.4 us
  starting transfers between devices: 37.2 us -> 7.27 us
  matrix products: 32.3 us -> 52.5 us
  other arithmetic: 30.4 us -> 13.6 us
  local copies, waits for them, and re-layouts: 25.1 us -> 19.5 us
    psum x0 -> x7, waiting for transfers between devices: none -> 251 us  [the longest x4 130 us: on_device(): lax.psum((jnp.sum(widened * widened, axis=-1, keepdims=True), product), '...]
    ppermute x12 -> x0, waiting for transfers between devices: 109 us -> none  [passed_along(): lax.ppermute(value, axis, [(source, source + steps) for source in range(i...]
    ppermute x12 -> x0, starting transfers between devices: 37.2 us -> none  [passed_along(): lax.ppermute(value, axis, [(source, source + steps) for source in range(i...]
    psum x1 -> x5, blocking collectives: 10.4 us -> 45.8 us  [the longest x4 36.7 us: on_device(): lax.psum((jnp.sum(widened * widened, axis=-1, keepdims=True), product), '...]
    dot_general x34 -> x40, matrix products: 32.3 us -> 52.5 us  [the longest x22 28.2 us: dot_nt(): lax.dot_general(left, right, (((1,), (1,)), ((), ())), preferred_element_...]
    all_to_all x0 -> x1, blocking collectives: none -> 13.6 us  [on_device(): low = lax.all_to_all(low.transpose(0, 2, 1, 3), 'section', 0, 0, tiled=True)]
    dynamic_update_slice x35 -> x0, other arithmetic: 13.4 us -> none  [keep_block(): lax.dynamic_update_index_in_dim(buffer, jnp.where(usable, element, before...]
    all_gather x1, waiting for transfers between devices: 40.2 us -> 27.1 us  [on_device(): low = lax.all_gather(low, 'dp', axis=2, tiled=True)]
  transfers between devices with their start and end apart: 14 -> 11, of which waited for: 14 -> 10; matrix products, arithmetic and copies ran while one was open for 6% -> 7% of each run, Pallas kernels for 0% -> 0%
where the time goes in v1:
time: 503 us; the launch traced here: 501 us
  waiting for transfers between devices  334 us (66%)
  blocking collectives  59.4 us (12%)
  matrix products  52.5 us (10%)
  local copies, waits for them, and re-layouts  19.5 us (4%)
  between operations  14.5 us (3%)
  other arithmetic  13.6 us (3%)
  starting transfers between devices  7.27 us (1%)
    psum x4, waiting for transfers between devices, on_device(): lax.psum((jnp.sum(widened * widened, axis=-1, keepdims=True), product), '...  130 us
    psum x3, waiting for transfers between devices, on_device(): lax.psum(jnp.dot(grad_out, up, preferred_element_type=jnp.float32), 'sect...  121 us
    reduce_scatter x1, waiting for transfers between devices, on_device(): gradient = lax.psum_scatter(gradient, 'dp', scatter_dimension=2, tiled=True)  50.1 us
    psum x4, blocking collectives, on_device(): lax.psum((jnp.sum(widened * widened, axis=-1, keepdims=True), product), '...  36.7 us
    dot_general x22, matrix products, dot_nt(): lax.dot_general(left, right, (((1,), (1,)), ((), ())), preferred_element_...  28.2 us
    all_gather x1, waiting for transfers between devices, on_device(): low = lax.all_gather(low, 'dp', axis=2, tiled=True)  27.1 us
    unnamed x68, local copies, waits for them, and re-layouts  14.8 us
    all_to_all x1, blocking collectives, on_device(): low = lax.all_to_all(low.transpose(0, 2, 1, 3), 'section', 0, 0, tiled=True)  13.6 us
  transfers between devices with their start and end apart: 11, of which 10 were waited for; matrix products, arithmetic and copies ran while one was open for 7% of the time, Pallas kernels for 0%

profile of v1, /device:TPU:0, one launch (start us, length us, event | category | flops | bytes accessed | tf_op | source)
XLA Modules:
  0.0 501.2 jit_solution(14029739731432798612)
XLA Ops:
  8.6 13.6 %all_to_all.19 = bf16[4,2,128,256]{3,2,1,0:T(8,128)(2,1)} all-to-all(bf16[4,2,128,256]{3,2,1,0:T(8,128)(2,1)S(1)} %copy.73), channel_id=1, replica_groups=mesh['section'=4,'dp'=8] {'section'}, dimensions={0} | all-to-all | bytes 1048576 | tf_op jit(solution)/shard_map/all_to_all | solution.py:48
  22.8 3.2 all-to-all-start
  26.1 3.3 copy.66
  29.6 4.0 copy.70
  34.1 2.1 broadcast_multiply_fusion
  42.1 27.1 %all-gather.2.cloned.1.call-done = bf16[4,2,1024,256]{3,2,1,0:T(8,128)(2,1)} async-done(((bf16[4,2,128,256]{3,2,1,0:T(8,128)(2,1)}), bf16[4,2,1024,256]{3,2,1,0:T(8,128)(2,1)}) %all-gather.2.cloned.1.call-update) | async-done | bytes 4194320 | tf_op jit(solution)/shard_map/all_gather | solution.py:49
  69.3 2.2 fusion.43
  71.6 2.4 convolution_bitcast_fusion
  73.9 9.8 %psum.93 = f32[256,1]{0,1:T(1,128)S(1)} all-reduce(f32[256,1]{0,1:T(1,128)S(1)} %bitcast.169), channel_id=1, replica_groups=mesh['section'=4,'dp'=8] {'section'}, use_global_device_ids=true, to_apply=%region_3.4 | all-reduce | flops 256 | bytes 2048 | tf_op jit(solution)/shard_map/psum | solution.py:68
  83.7 30.6 %all-reduce.9.cloned.1.call-done = f32[256,256]{1,0:T(8,128)} async-done(((f32[256,256]{1,0:T(8,128)}), f32[256,256]{1,0:T(8,128)}) %all-reduce.9.cloned.1.call-update) | async-done | bytes 262160 | tf_op jit(solution)/shard_map/psum | solution.py:68
  115.9 2.2 fusion.53
  118.2 2.1 fusion.44
  120.3 9.0 %psum.95 = f32[256,1]{0,1:T(1,128)S(1)} all-reduce(f32[256,1]{0,1:T(1,128)S(1)} %bitcast.194), channel_id=1, replica_groups=mesh['section'=4,'dp'=8] {'section'}, use_global_device_ids=true, to_apply=%region_6.7 | all-reduce | flops 256 | bytes 2048 | tf_op jit(solution)/shard_map/psum | solution.py:68
  129.3 32.0 %all-reduce.11.cloned.1.call-done = f32[256,256]{1,0:T(8,128)} async-done(((f32[256,256]{1,0:T(8,128)}), f32[256,256]{1,0:T(8,128)}) %all-reduce.11.cloned.1.call-update) | async-done | bytes 262160 | tf_op jit(solution)/shard_map/psum | solution.py:68
  162.9 2.2 fusion.55
  166.3 8.9 %psum.97 = f32[256,1]{0,1:T(1,128)S(1)} all-reduce(f32[256,1]{0,1:T(1,128)S(1)} %bitcast.195), channel_id=1, replica_groups=mesh['section'=4,'dp'=8] {'section'}, use_global_device_ids=true, to_apply=%region_9.10 | all-reduce | flops 256 | bytes 2048 | tf_op jit(solution)/shard_map/psum | solution.py:68
  175.3 33.1 %all-reduce.13.cloned.1.call-done = f32[256,256]{1,0:T(8,128)} async-done(((f32[256,256]{1,0:T(8,128)}), f32[256,256]{1,0:T(8,128)}) %all-reduce.13.cloned.1.call-update) | async-done | bytes 262160 | tf_op jit(solution)/shard_map/psum | solution.py:68
  210.7 2.1 fusion.57
  213.2 9.0 %psum.99 = f32[256,1]{0,1:T(1,128)S(1)} all-reduce(f32[256,1]{0,1:T(1,128)S(1)} %bitcast.193), channel_id=1, replica_groups=mesh['section'=4,'dp'=8] {'section'}, use_global_device_ids=true, to_apply=%region_12.13 | all-reduce | flops 256 | bytes 2048 | tf_op jit(solution)/shard_map/psum | solution.py:68
  223.9 34.5 %all-reduce.21.cloned.1.call-done = (f32[256,256]{1,0:T(8,128)}, f32[256,256]{1,0:T(8,128)}) async-done(((f32[256,256]{1,0:T(8,128)}, f32[256,256]{1,0:T(8,128)}), (f32[256,256]{1,0:T(8,128)}, f32[256,256]{1,0:T(8,128)})) %all-reduce.21.cloned.1.call-update) | async-done | bytes 524304 | tf_op jit(solution)/shard_map/psum | solution.py:68
  263.9 2.1 fusion.56
  267.5 41.5 %all-reduce.15.cloned.1.call-done = f32[256,256]{1,0:T(8,128)} async-done(((f32[256,256]{1,0:T(8,128)}), f32[256,256]{1,0:T(8,128)}) %all-reduce.15.cloned.1.call-update) | async-done | bytes 262160 | tf_op jit(solution)/shard_map/psum | solution.py:83
  311.9 2.1 fusion.54
  316.3 40.7 %all-reduce.17.cloned.1.call-done = f32[256,256]{1,0:T(8,128)} async-done(((f32[256,256]{1,0:T(8,128)}), f32[256,256]{1,0:T(8,128)}) %all-reduce.17.cloned.1.call-update) | async-done | bytes 262160 | tf_op jit(solution)/shard_map/psum | solution.py:83
  360.0 2.1 fusion.52
  363.4 2.2 fusion.22
  366.7 38.5 %all-reduce.19.cloned.1.call-done = f32[256,256]{1,0:T(8,128)} async-done(((f32[256,256]{1,0:T(8,128)}), f32[256,256]{1,0:T(8,128)}) %all-reduce.19.cloned.1.call-update) | async-done | bytes 262160 | tf_op jit(solution)/shard_map/psum | solution.py:83
  409.3 9.1 %psum.103 = f32[2]{0:T(128)S(1)} all-reduce(f32[2]{0:T(128)S(1)} %fusion.28), channel_id=1, replica_groups=mesh['section'=4,'dp'=8] {'section'}, use_global_device_ids=true, to_apply=%region_20.21 | all-reduce | flops 2 | bytes 16 | tf_op jit(solution)/shard_map/psum | solution.py:103
  425.8 2.2 pad_maximum_fusion
  428.1 50.1 %reduce-scatter.2.cloned.1.call-done = bf16[4,2,128,256]{3,2,1,0:T(8,128)(2,1)} async-done(((bf16[4,2,1024,256]{3,2,1,0:T(8,128)(2,1)}), bf16[4,2,128,256]{3,2,1,0:T(8,128)(2,1)}) %reduce-scatter.2.cloned.1.call-update) | async-done | bytes 524304 | tf_op jit(solution)/shard_map/reduce_scatter | solution.py:115
  478.2 3.7 all-to-all-start.2
  482.4 6.1 %all-to-all-done.2 = bf16[4,2,128,256]{3,2,1,0:T(8,128)(2,1)S(1)} async-done(((bf16[4,2,128,256]{3,2,1,0:T(8,128)(2,1)}), bf16[4,2,128,256]{3,2,1,0:T(8,128)(2,1)S(1)}, u32[]{:S(2)}, u32[]{:S(2)}) %all-to-all-start.2) | async-done | bytes 524320 | tf_op jit(solution)/shard_map/all_to_all | solution.py:116
  (145 shorter events, 53.0 us)
Async XLA Ops:
  7.2 62.1 %all-gather.2.cloned.1.call-start = ((), (), s32[]{:S(2)}) async-start(), calls=%async_computation.4 | async-start | bytes 4718592 | tf_op jit(solution)/shard_map/all_gather | solution.py:49
  22.8 18.3 %all-to-all-start = ((f32[4,1,1024]{2,1,0:T(1,128)}), f32[4,1,1024]{2,1,0:T(1,128)S(1)}, u32[]{:S(2)}, u32[]{:S(2)}) async-start(f32[4,1,1024]{2,1,0:T(1,128)} %bitcast.4), calls=%async_computation | async-start | bytes 32768 | tf_op jit(solution)/shard_map/all_to_all | solution.py:51
  26.0 88.3 %all-reduce.9.cloned.1.call-start = ((), (), s32[]{:S(2)}) async-start(), calls=%async_computation.5 | async-start | bytes 524288 | tf_op jit(solution)/shard_map/psum | solution.py:68
  41.1 124.2 %copy-start.13 = (f32[1,1,1024]{2,1,0:T(1,128)}, f32[1,1,1024]{2,1,0:T(1,128)S(1)}, u32[]{:S(2)}) copy-start(f32[1,1,1024]{2,1,0:T(1,128)S(1)} %get-tuple-element.43) | copy-start | bytes 12292
  41.1 171.8 %copy-start.18 = (f32[1,1,1024]{2,1,0:T(1,128)}, f32[1,1,1024]{2,1,0:T(1,128)S(1)}, u32[]{:S(2)}) copy-start(f32[1,1,1024]{2,1,0:T(1,128)S(1)} %get-tuple-element.42) | copy-start | bytes 12292
  41.1 181.2 %copy-start.16 = (f32[1,1,1024]{2,1,0:T(1,128)}, f32[1,1,1024]{2,1,0:T(1,128)S(1)}, u32[]{:S(2)}) copy-start(f32[1,1,1024]{2,1,0:T(1,128)S(1)} %get-tuple-element.41) | copy-start | bytes 12292
  42.1 76.1 %copy-start.3 = (bf16[256,8,1,128]{0,3,2,1:T(8,128)(2,1)S(1)}, bf16[256,8,1,128]{0,3,2,1:T(8,128)(2,1)}, u32[]{:S(2)}) copy-start(bf16[256,8,1,128]{0,3,2,1:T(8,128)(2,1)} %get-tuple-element.29) | copy-start | bytes 1572868
  71.5 89.8 %all-reduce.11.cloned.1.call-start = ((), (), s32[]{:S(2)}) async-start(), calls=%async_computation.6 | async-start | bytes 524288 | tf_op jit(solution)/shard_map/psum | solution.py:68
  115.9 50.5 %copy-start.27 = (bf16[256,1024]{1,0:T(8,128)(2,1)}, bf16[256,1024]{1,0:T(8,128)(2,1)S(1)}, u32[]{:S(2)}) copy-start(bf16[256,1024]{1,0:T(8,128)(2,1)S(1)} %get-tuple-element.46) | copy-start | bytes 1572868
  118.2 90.1 %all-reduce.13.cloned.1.call-start = ((), (), s32[]{:S(2)}) async-start(), calls=%async_computation.7 | async-start | bytes 524288 | tf_op jit(solution)/shard_map/psum | solution.py:68
  162.9 50.3 %copy-start.29 = (bf16[256,1024]{1,0:T(8,128)(2,1)}, bf16[256,1024]{1,0:T(8,128)(2,1)S(1)}, u32[]{:S(2)}) copy-start(bf16[256,1024]{1,0:T(8,128)(2,1)S(1)} %get-tuple-element.48) | copy-start | bytes 1572868
  165.2 93.2 %all-reduce.21.cloned.1.call-start = ((), (), s32[]{:S(2)}) async-start(), calls=%async_computation.12 | async-start | bytes 1048576 | tf_op jit(solution)/shard_map/psum | solution.py:68
  175.3 139.0 %copy-start.9 = (f32[256,1]{0,1:T(1,128)}, f32[256,1]{0,1:T(1,128)S(1)}, u32[]{:S(2)}) copy-start(f32[256,1]{0,1:T(1,128)S(1)} %add_rsqrt_fusion.1) | copy-start | bytes 3076
  209.9 52.3 %copy-start.2 = (bf16[256,1024]{1,0:T(8,128)(2,1)S(1)}, bf16[256,1024]{1,0:T(8,128)(2,1)}, u32[]{:S(2)}) copy-start(bf16[256,1024]{1,0:T(8,128)(2,1)} %copy.88) | copy-start | bytes 1572868
  209.9 52.3 %copy-start.22 = (bf16[256]{0:T(256)(128)(2,1)S(1)}, bf16[256]{0:T(256)(128)(2,1)}, u32[]{:S(2)}) copy-start(bf16[256]{0:T(256)(128)(2,1)} %copy-done.21) | copy-start | bytes 1540
  212.8 96.2 %all-reduce.15.cloned.1.call-start = ((), (), s32[]{:S(2)}) async-start(), calls=%async_computation.8 | async-start | bytes 524288 | tf_op jit(solution)/shard_map/psum | solution.py:83
  259.8 49.2 %copy-start.6 = (f32[256,256]{1,0:T(8,128)S(1)}, f32[256,256]{1,0:T(8,128)}, u32[]{:S(2)}) copy-start(f32[256,256]{1,0:T(8,128)} %all-reduce.13.cloned.1.call-done) | copy-start | bytes 786436
  261.2 49.1 %copy-start.19 = (f32[1,1,1024]{2,1,0:T(1,128)S(1)}, f32[1,1,1024]{2,1,0:T(1,128)}, u32[]{:S(2)}) copy-start(f32[1,1,1024]{2,1,0:T(1,128)} %copy-done.18) | copy-start | bytes 12292
  266.0 91.1 %all-reduce.17.cloned.1.call-start = ((), (), s32[]{:S(2)}) async-start(), calls=%async_computation.9 | async-start | bytes 524288 | tf_op jit(solution)/shard_map/psum | solution.py:83
  310.3 48.1 %copy-start.14 = (f32[1,1,1024]{2,1,0:T(1,128)S(1)}, f32[1,1,1024]{2,1,0:T(1,128)}, u32[]{:S(2)}) copy-start(f32[1,1,1024]{2,1,0:T(1,128)} %copy-done.13) | copy-start | bytes 12292
  314.0 91.2 %all-reduce.19.cloned.1.call-start = ((), (), s32[]{:S(2)}) async-start(), calls=%async_computation.10 | async-start | bytes 524288 | tf_op jit(solution)/shard_map/psum | solution.py:83
  316.3 88.9 %copy-start.4 = (f32[256,256]{1,0:T(8,128)S(1)}, f32[256,256]{1,0:T(8,128)}, u32[]{:S(2)}) copy-start(f32[256,256]{1,0:T(8,128)} %all-reduce.9.cloned.1.call-done) | copy-start | bytes 786436
  360.0 48.9 %copy-start.24 = (pred[256]{0:T(512)(128)(4,1)S(1)}, pred[256]{0:T(512)(128)(4,1)}, u32[]{:S(2)}) copy-start(pred[256]{0:T(512)(128)(4,1)} %get-tuple-element.32) | copy-start | bytes 772
  360.0 58.5 %copy-start.20 = (f32[1,1,1024]{2,1,0:T(1,128)S(1)}, f32[1,1,1024]{2,1,0:T(1,128)}, u32[]{:S(2)}) copy-start(f32[1,1,1024]{2,1,0:T(1,128)} %copy-done.18) | copy-start | bytes 12292
  362.1 57.9 %copy-start.12 = (f32[256,1]{0,1:T(1,128)S(1)}, f32[256,1]{0,1:T(1,128)}, u32[]{:S(2)}) copy-start(f32[256,1]{0,1:T(1,128)} %copy-done.11) | copy-start | bytes 3076
  362.1 57.9 %copy-start.23 = (bf16[256]{0:T(256)(128)(2,1)S(1)}, bf16[256]{0:T(256)(128)(2,1)}, u32[]{:S(2)}) copy-start(bf16[256]{0:T(256)(128)(2,1)} %copy-done.21) | copy-start | bytes 1540
  362.1 116.1 %reduce-scatter.2.cloned.1.call-start = ((), (), s32[]{:S(2)}) async-start(), calls=%async_computation.11 | async-start | bytes 4718592 | tf_op jit(solution)/shard_map/reduce_scatter | solution.py:115
  365.6 56.1 %copy-start.17 = (f32[1,1,1024]{2,1,0:T(1,128)S(1)}, f32[1,1,1024]{2,1,0:T(1,128)}, u32[]{:S(2)}) copy-start(f32[1,1,1024]{2,1,0:T(1,128)} %copy-done.16) | copy-start | bytes 12292
  366.6 56.5 %copy-start.15 = (f32[1,1,1024]{2,1,0:T(1,128)S(1)}, f32[1,1,1024]{2,1,0:T(1,128)}, u32[]{:S(2)}) copy-start(f32[1,1,1024]{2,1,0:T(1,128)} %copy-done.13) | copy-start | bytes 12292
  428.1 60.6 %copy-start = (f32[1,512,2,256]{3,2,1,0:T(2,128)S(1)}, f32[1,512,2,256]{3,2,1,0:T(2,128)}, u32[]{:S(2)}) copy-start(f32[1,512,2,256]{3,2,1,0:T(2,128)} %param.15) | copy-start | bytes 3145732
  428.1 60.6 %copy-start.1 = (f32[1,512,2,256]{3,2,1,0:T(2,128)S(1)}, f32[1,512,2,256]{3,2,1,0:T(2,128)}, u32[]{:S(2)}) copy-start(f32[1,512,2,256]{3,2,1,0:T(2,128)} %param.14) | copy-start | bytes 3145732
  478.2 10.2 %all-to-all-start.2 = ((bf16[4,2,128,256]{3,2,1,0:T(8,128)(2,1)}), bf16[4,2,128,256]{3,2,1,0:T(8,128)(2,1)S(1)}, u32[]{:S(2)}, u32[]{:S(2)}) async-start(bf16[4,2,128,256]{3,2,1,0:T(8,128)(2,1)} %reduce-scatter.2.cloned.1.call-done), calls=%async_computation.3 | async-start | bytes 1048576 | tf_op jit(solution)/shard_map/all_to_all | solution.py:116
  (10 other events, 119.0 us)
Sparse Core Ops, SparseCore 0:
  22.3 46.9 all-gather.1
  72.8 41.5 all-reduce.8
  118.3 43.0 all-reduce.10
  165.3 42.9 all-reduce.12
  212.9 45.4 all-reduce.20
  266.1 42.8 all-reduce.14
  314.1 42.9 all-reduce.16
  362.2 42.9 all-reduce.18
  428.2 49.9 reduce-scatter.1

commit v2 on v1

v2 whole, which is shorter than its diff:
```python
import functools

import jax
import jax.numpy as jnp
from jax import lax
from jax.experimental import pallas as pl
from jax.experimental.pallas import tpu as pltpu
from jax.sharding import PartitionSpec as P

SEQLEN = 64
USERS_DEV = 2


CLIP_BOUND = 70000.0
LOSS_SCALE = 1024.0
BETA_ONE = 0.9
BETA_TWO = 0.999
FIRST_FIX = 1.0 - 0.9**50
SECOND_FIX = 1.0 - 0.999**50
ADAM_EPS = 1e-08
NORM_EPS = 1e-05
LANES = 128


def dot_nt(left, right):
    return lax.dot_general(
        left, right, (((1,), (1,)), ((), ())), preferred_element_type=jnp.float32
    )


def dot_tn(left, right):
    return lax.dot_general(
        left, right, (((0,), (0,)), ((), ())), preferred_element_type=jnp.float32
    )


def split_lanes(column, rows):
    wide = jnp.broadcast_to(column, (rows, LANES))
    high = wide.astype(jnp.bfloat16).astype(jnp.float32)
    lane = lax.broadcasted_iota(jnp.int32, (rows, LANES), 1)
    return jnp.where(lane < LANES // 2, high, wide - high).astype(jnp.bfloat16)


def joined_lanes(block, start):
    high = block[:, start : start + 1].astype(jnp.float32)
    return high + block[:, start + LANES // 2 : start + LANES // 2 + 1].astype(jnp.float32)


def chain_kernel(
    sections,
    model_width,
    tokens_ref,
    cotangent_ref,
    gains_ref,
    owners_ref,
    owners_row_ref,
    low_ref,
    gradient_ref,
    norm_ref,
    hidden,
    scaled,
    grad_out,
    active,
    grad_scaled,
    inner,
    inverse,
    own_part,
    outgoing,
    landed,
    joint,
    squares,
    send_sem,
    recv_sem,
):
    me = lax.axis_index("section")
    tok_rows, held = tokens_ref.shape
    width = active.shape[2]
    block = tok_rows // sections
    own = pl.ds(pl.multiple_of(me * block, block), block)
    peers = [lax.rem(me + d, sections) for d in range(1, sections)]

    barrier = pltpu.get_barrier_semaphore()
    for peer in peers:
        pl.semaphore_signal(
            barrier, inc=1, device_id={"section": peer}, device_id_type=pl.DeviceIdType.MESH
        )
    pl.semaphore_wait(barrier, sections - 1)

    def copies(make, slot):
        return [
            pltpu.make_async_remote_copy(
                src_ref=source,
                dst_ref=target,
                send_sem=send_sem.at[slot, d],
                recv_sem=recv_sem.at[slot, d],
                device_id={"section": peers[d]},
                device_id_type=pl.DeviceIdType.MESH,
            )
            for d in range(sections - 1)
            for source, target in [make(d)]
        ]

    def to_owners(step):
        def make(d):
            rows = pl.ds(pl.multiple_of(peers[d] * block, block), block)
            return outgoing.at[step, rows], landed.at[step, d]

        return copies(make, 2 * step)

    def to_all(ref, s, step):
        def make(d):
            return ref.at[s, own], ref.at[s, own]

        return copies(make, 2 * step + 1)

    def start(sent):
        for copy in sent:
            copy.start()

    def arrived(sent):
        for copy in sent:
            copy.wait_recv()

    hidden[0] = tokens_ref[...]
    joint[...] = jnp.zeros_like(joint)

    def forward(s, carry):
        widened = hidden[s].astype(jnp.float32)
        now = (widened * gains_ref[s]).astype(jnp.bfloat16)
        scaled[s] = now
        product = jnp.dot(now, low_ref[s, 0], preferred_element_type=jnp.float32)
        square = jnp.sum(widened * widened, axis=-1, keepdims=True)
        own_part[:, :width] = product
        own_part[:, width:] = jnp.broadcast_to(square, (tok_rows, LANES))
        outgoing[s, :, :width] = product.astype(jnp.bfloat16)
        outgoing[s, :, width:] = split_lanes(square, tok_rows)
        sent = to_owners(s)
        start(sent)
        arrived(sent)
        total = own_part[own, :width]
        mean = own_part[own, width : width + 1]
        for d in range(sections - 1):
            piece = landed[s, d]
            total = total + piece[:, :width].astype(jnp.float32)
            mean = mean + joined_lanes(piece, width)
        scale = lax.rsqrt(mean / model_width + NORM_EPS)
        value = total * scale
        inner[s] = value
        inverse[s] = jnp.broadcast_to(scale, (block, LANES))
        active[s, own] = (value / (1.0 + jnp.exp(-value))).astype(jnp.bfloat16)
        sent = to_all(active, s, s)
        start(sent)
        arrived(sent)

        @pl.when(s < sections - 1)
        def _():
            branch = dot_nt(active[s], low_ref[s, 1])
            hidden[s + 1] = (hidden[s].astype(jnp.float32) + branch).astype(jnp.bfloat16)

        return carry

    lax.fori_loop(0, sections, forward, 0)
    grad_out[sections - 1] = cotangent_ref[...]

    def backward(back, carry):
        s = sections - 1 - back
        step = sections + back
        product = jnp.dot(grad_out[s], low_ref[s, 1], preferred_element_type=jnp.float32)
        own_part[:, :width] = product
        outgoing[step, :, :width] = product.astype(jnp.bfloat16)
        sent = to_owners(step)
        start(sent)
        joint[...] += dot_nt(active[s], active[s]) * dot_nt(grad_out[s], grad_out[s])
        arrived(sent)
        total = own_part[own, :width]
        for d in range(sections - 1):
            total = total + landed[step, d, :, :width].astype(jnp.float32)
        value = inner[s]
        scale = inverse[s][:, :1]
        sigmoid_val = 1.0 / (1.0 + jnp.exp(-value))
        grad_inner = total * sigmoid_val * (1.0 + value * (1.0 - sigmoid_val))
        pull = jnp.sum(grad_inner * value, axis=-1, keepdims=True) * (
            scale * scale / model_width
        )
        grad_scaled[s, own, :width] = (grad_inner * scale).astype(jnp.bfloat16)
        grad_scaled[s, own, width:] = split_lanes(pull, block)
        sent = to_all(grad_scaled, s, step)
        start(sent)
        gram = dot_nt(scaled[s], scaled[s])
        arrived(sent)
        whole = grad_scaled[s]
        low_grad = whole[:, :width]

        @pl.when(s > 0)
        def _():
            grad_out[s - 1] = (
                grad_out[s].astype(jnp.float32)
                + gains_ref[s] * dot_nt(low_grad, low_ref[s, 0])
                - hidden[s].astype(jnp.float32) * joined_lanes(whole, width)
            ).astype(jnp.bfloat16)

        joint[...] += gram * dot_nt(low_grad, low_grad)
        return carry

    lax.fori_loop(0, sections, backward, 0)

    row_of = lax.broadcasted_iota(jnp.int32, (8, LANES), 0)
    sums = jnp.zeros((8, LANES), jnp.float32)
    for user in range(USERS_DEV):
        spread = joint[...] * owners_row_ref[user : user + 1, :]
        held_sum = jnp.sum(spread, axis=-1, keepdims=True) * owners_ref[:, user : user + 1]
        whole_sum = jnp.sum(held_sum, axis=0, keepdims=True)
        sums = jnp.where(row_of == user, whole_sum, sums)
    squares[me] = sums
    sent = copies(lambda d: (squares.at[me], squares.at[me]), 4 * sections)
    start(sent)
    arrived(sent)
    total = squares[0]
    for s in range(1, sections):
        total = total + squares[s]
    user_norm = jnp.sqrt(total)
    norm_ref[...] = user_norm
    factors = LOSS_SCALE / jnp.maximum(user_norm, CLIP_BOUND)
    token_factor = owners_ref[:, :1] * factors[:1, :1]
    for user in range(1, USERS_DEV):
        token_factor = token_factor + owners_ref[:, user : user + 1] * factors[user : user + 1, :1]

    def products(s, carry):
        weighted_inner = (grad_scaled[s, :, :width].astype(jnp.float32) * token_factor).astype(
            jnp.bfloat16
        )
        weighted_out = (grad_out[s].astype(jnp.float32) * token_factor).astype(jnp.bfloat16)
        gradient_ref[s, 0] = dot_tn(scaled[s], weighted_inner).astype(jnp.bfloat16)
        gradient_ref[s, 1] = dot_tn(weighted_out, active[s]).astype(jnp.bfloat16)
        return carry

    lax.fori_loop(0, sections, products, 0)

    def drain(step, carry):
        for copy in to_owners(step) + to_all(active, 0, step):
            copy.wait_send()
        return carry

    def drain_back(step, carry):
        for copy in to_owners(step) + to_all(grad_scaled, 0, step):
            copy.wait_send()
        return carry

    lax.fori_loop(0, sections, drain, 0)
    lax.fori_loop(sections, 2 * sections, drain_back, 0)
    for copy in sent:
        copy.wait_send()


def chain(tokens, cotangent, gains, owners, low, model_width):
    sections, _, held, width = low.shape
    tok_rows = tokens.shape[0]
    block = tok_rows // sections
    vmem = pl.BlockSpec(memory_space=pltpu.VMEM)
    owners_row = jnp.pad(owners.T, ((0, 8 - USERS_DEV), (0, 0)))
    owners = jnp.pad(owners, ((0, 0), (0, LANES - USERS_DEV)))
    steps = 2 * sections
    copies = (2 * steps + 1, sections - 1)
    bf16, f32 = jnp.bfloat16, jnp.float32
    return pl.pallas_call(
        functools.partial(chain_kernel, sections, model_width),
        out_shape=(
            jax.ShapeDtypeStruct(low.shape, bf16),
            jax.ShapeDtypeStruct((8, LANES), f32),
        ),
        in_specs=[vmem] * 6,
        out_specs=(vmem, vmem),
        scratch_shapes=[
            pltpu.VMEM((sections, tok_rows, held), bf16),
            pltpu.VMEM((sections, tok_rows, held), bf16),
            pltpu.VMEM((sections, tok_rows, held), bf16),
            pltpu.VMEM((sections, tok_rows, width), bf16),
            pltpu.VMEM((sections, tok_rows, width + LANES), bf16),
            pltpu.VMEM((sections, block, width), f32),
            pltpu.VMEM((sections, block, LANES), f32),
            pltpu.VMEM((tok_rows, width + LANES), f32),
            pltpu.VMEM((steps, tok_rows, width + LANES), bf16),
            pltpu.VMEM((steps, sections - 1, block, width + LANES), bf16),
            pltpu.VMEM((tok_rows, tok_rows), f32),
            pltpu.VMEM((sections, 8, LANES), f32),
            pltpu.SemaphoreType.DMA(copies),
            pltpu.SemaphoreType.DMA(copies),
        ],
        compiler_params=pltpu.CompilerParams(
            collective_id=0, has_side_effects=True, vmem_limit_bytes=48 * 1024 * 1024
        ),
    )(tokens, cotangent, gains[:, None, :], owners, owners_row, low)


def on_device(
    tokens, cotangent, lengths, seq_user, norm_gains, weights, first_moment, second_moment
):
    sections = lax.axis_size("section")
    quarter = lax.axis_index("section")
    shards = lax.axis_size("dp")
    tok_rows, model_width = tokens.shape
    own_rows, _, width = weights.shape[1:]
    part = own_rows // sections
    held = shards * part

    def own_features(values):
        split = values.reshape(tok_rows, shards, sections, part)
        return lax.dynamic_index_in_dim(split, quarter, 2, keepdims=False).reshape(tok_rows, held)

    low = weights[0].astype(jnp.bfloat16).reshape(sections, part, 2, width)
    low = lax.all_to_all(low.transpose(0, 2, 1, 3), "section", 0, 0, tiled=True)
    low = lax.all_gather(low, "dp", axis=2, tiled=True)
    gains = norm_gains[0].reshape(shards, sections, part).transpose(1, 0, 2)
    gains = lax.all_to_all(gains.reshape(sections, held), "section", 0, 0, tiled=True)

    positions = jnp.arange(tok_rows) % SEQLEN
    usable = positions < jnp.repeat(lengths, SEQLEN)
    local_user = seq_user - lax.axis_index("dp") * USERS_DEV
    token_user = jnp.repeat(local_user, SEQLEN)
    owners = ((token_user[:, None] == jnp.arange(USERS_DEV)[None, :]) & usable[:, None]).astype(
        jnp.float32
    )

    seeds = own_features(cotangent) * usable[:, None].astype(jnp.bfloat16)
    gradient, norms = chain(own_features(tokens), seeds, gains, owners, low, model_width)
    user_norm = norms[:USERS_DEV, 0]
    gradient = lax.psum_scatter(gradient, "dp", scatter_dimension=2, tiled=True)
    gradient = lax.all_to_all(gradient, "section", 0, 0, tiled=True)
    gradient = gradient.transpose(0, 2, 1, 3).reshape(own_rows, 2, width).astype(jnp.float32)
    moment_one = BETA_ONE * first_moment[0] + (1.0 - BETA_ONE) * gradient
    moment_two = BETA_TWO * second_moment[0] + (1.0 - BETA_TWO) * gradient * gradient
    direction = moment_one / FIRST_FIX / (jnp.sqrt(moment_two / SECOND_FIX) + ADAM_EPS)
    return (moment_one[None], moment_two[None], direction[None], user_norm / CLIP_BOUND)


def solution(mesh):
    return jax.shard_map(
        on_device,
        mesh=mesh,
        in_specs=(
            P("dp", None),
            P("dp", None),
            P("dp"),
            P("dp"),
            P("section", None),
            P("section", "dp", None, None),
            P("section", "dp", None, None),
            P("section", "dp", None, None),
        ),
        out_specs=(
            P("section", "dp", None, None),
            P("section", "dp", None, None),
            P("section", "dp", None, None),
            P("dp"),
        ),
        check_vma=False,
    )
```

time: 503 us -> 226 us (0.45)
  waiting for transfers between devices: 334 us -> 81 us
  Pallas kernels: 0 us -> 82.5 us
  matrix products: 52.5 us -> 0 us
  blocking collectives: 59.4 us -> 13.6 us
  other arithmetic: 13.6 us -> 1.67 us
  local copies, waits for them, and re-layouts: 19.5 us -> 25.2 us
    psum x7 -> x0, waiting for transfers between devices: 251 us -> none  [the longest x4 130 us: on_device(): lax.psum((jnp.sum(widened * widened, axis=-1, keepdims=True), product), '...]
    pallas_call x0 -> x1, Pallas kernels: none -> 82.5 us  [chain(): pl.pallas_call(functools.partial(chain_kernel, sections, model_width), ou...]
    dot_general x40 -> x0, matrix products: 52.5 us -> none  [the longest x22 28.2 us: dot_nt(): lax.dot_general(left, right, (((1,), (1,)), ((), ())), preferred_element_...]
    psum x5 -> x0, blocking collectives: 45.8 us -> none  [the longest x4 36.7 us: on_device(): lax.psum((jnp.sum(widened * widened, axis=-1, keepdims=True), product), '...]
    dynamic_slice x0 -> x1, local copies, waits for them, and re-layouts: none -> 7.77 us  [own_features(): lax.dynamic_index_in_dim(split, quarter, 2, keepdims=False)]
    unnamed x68 -> x17, local copies, waits for them, and re-layouts: 14.8 us -> 8.67 us
    reshape x1 -> x2, local copies, waits for them, and re-layouts: 2.05 us -> 7.75 us  [own_features(): split = values.reshape(tok_rows, shards, sections, part)]
  transfers between devices with their start and end apart: 11 -> 4, of which waited for: 10 -> 3; matrix products, arithmetic and copies ran while one was open for 7% -> 8% of each run, Pallas kernels for 0% -> 0%
where the time goes in v2:
time: 226 us; the launch traced here: 225 us
  Pallas kernels  82.5 us (37%)
  waiting for transfers between devices  81 us (36%)
  local copies, waits for them, and re-layouts  25.2 us (11%)
  between operations  14.3 us (6%)
  blocking collectives  13.6 us (6%)
  starting transfers between devices  6.98 us (3%)
    pallas_call x1, Pallas kernels, chain(): pl.pallas_call(functools.partial(chain_kernel, sections, model_width), ou...  82.5 us
    reduce_scatter x1, waiting for transfers between devices, on_device(): gradient = lax.psum_scatter(gradient, 'dp', scatter_dimension=2, tiled=True)  48.3 us
    all_gather x1, waiting for transfers between devices, on_device(): low = lax.all_gather(low, 'dp', axis=2, tiled=True)  26.8 us
    all_to_all x1, blocking collectives, on_device(): low = lax.all_to_all(low.transpose(0, 2, 1, 3), 'section', 0, 0, tiled=True)  13.6 us
    unnamed x17, local copies, waits for them, and re-layouts  8.67 us
    dynamic_slice x1, local copies, waits for them, and re-layouts, own_features(): lax.dynamic_index_in_dim(split, quarter, 2, keepdims=False)  7.77 us
    reshape x2, local copies, waits for them, and re-layouts, own_features(): split = values.reshape(tok_rows, shards, sections, part)  7.75 us
    all_to_all x1, waiting for transfers between devices, on_device(): gradient = lax.all_to_all(gradient, 'section', 0, 0, tiled=True)  5.91 us
  transfers between devices with their start and end apart: 4, of which 3 were waited for; matrix products, arithmetic and copies ran while one was open for 8% of the time, Pallas kernels for 0%

profile of v2, /device:TPU:0, one launch (start us, length us, event | category | flops | bytes accessed | tf_op | source)
XLA Modules:
  0.0 225.3 jit_solution(15737398540260600118)
XLA Ops:
  7.2 0.0 all-gather.2.cloned.1.call-start
  7.2 1.3 copy.40
  8.6 13.6 %all_to_all.19 = bf16[4,2,128,256]{3,2,1,0:T(8,128)(2,1)} all-to-all(bf16[4,2,128,256]{3,2,1,0:T(8,128)(2,1)S(1)} %bitcast.26), channel_id=1, replica_groups=mesh['section'=4,'dp'=8] {'section'}, dimensions={0} | all-to-all | bytes 1048576 | tf_op jit(solution)/shard_map/all_to_all | solution.py:311
  22.2 0.0 all-gather.2.cloned.1.call-update
  22.2 0.6 copy.18
  22.8 3.3 %all-to-all-start = ((f32[4,1,1024]{2,1,0:T(1,128)}), f32[4,1,1024]{2,1,0:T(1,128)S(1)}, u32[]{:S(2)}, u32[]{:S(2)}) async-start(f32[4,1,1024]{2,1,0:T(1,128)} %bitcast.2), calls=%async_computation | async-start | bytes 32768 | tf_op jit(solution)/shard_map/all_to_all | solution.py:314
  26.1 0.0 reduce-scatter.2.cloned.1.call-start
  26.1 0.1 broadcast_in_dim.5
  26.2 0.1 eq.24
  26.3 0.1 broadcast_in_dim.4
  26.4 0.1 reshape.88
  26.5 3.3 %reshape.84 = bf16[256,8,4,128]{3,2,1,0:T(4,128)(2,1)S(1)} reshape(bf16[256,4096]{1,0:T(8,128)(2,1)} %param.8) | data formatting | bytes 4194304 | tf_op jit(solution)/shard_map/reshape | solution.py:307
  29.7 4.5 %reshape.86 = bf16[256,8,4,128]{3,2,1,0:T(4,128)(2,1)} reshape(bf16[256,4096]{1,0:T(8,128)(2,1)} %param.9) | data formatting | bytes 4194304 | tf_op jit(solution)/shard_map/reshape | solution.py:307
  34.2 0.1 fusion.2
  34.4 7.8 %dynamic-slice_reduce_fusion = (bf16[256,8,128]{2,1,0:T(8,128)(2,1)S(1)}, bf16[256,8,128]{2,1,0:T(8,128)(2,1)S(1)}) fusion(bf16[256,8,4,128]{3,2,1,0:T(4,128)(2,1)} %reshape.86, s32[]{:T(128)S(6)} %select_n.19, bf16[256,8,4,128]{3,2,1,0:T(4,128)(2,1)S(1)} %reshape.84), kind=kLoop, calls=%fused_computation.9 | loop fusion | bytes 2097156 | tf_op jit(solution)/shard_map/jit(dynamic_index_in_dim)/dynamic_slice | solution.py:308
  42.2 0.1 bitcast_multiply_fusion.1.cotangent_ref
  42.3 0.1 copy.43
  42.4 26.8 %all-gather.2.cloned.1.call-done.low_ref = bf16[4,2,1024,256]{3,2,1,0:T(8,128)(2,1)} async-done(((bf16[4,2,128,256]{3,2,1,0:T(8,128)(2,1)}), bf16[4,2,1024,256]{3,2,1,0:T(8,128)(2,1)}) %all-gather.2.cloned.1.call-update) | async-done | bytes 4194320 | tf_op jit(solution)/shard_map/all_gather | solution.py:312
  69.2 82.5 %shard_map.111 = (bf16[4,2,1024,256]{3,2,1,0:T(8,128)(2,1)S(1)}, f32[8,128]{1,0:T(8,128)S(1)}) custom-call(bf16[256,1024]{1,0:T(8,128)(2,1)S(1)} %bitcast.24, bf16[256,1024]{1,0:T(8,128)(2,1)S(1)} %bitcast_multiply_fusion.1.cotangent_ref, f32[4,1,1024]{2,1,0:T(1,128)S(1)} %all-to-all-done.gains_ref, f32[256,128]{1,0:T(8,128)S(1)} %pad_convert_fusion.owners_ref, ...), custom_call_target="tpu_custom_call" | custom-call | tf_op jit(solution)/shard_map/pallas_call | solution.py:265
  151.7 1.9 copy-done
  153.7 0.0 reduce-scatter.2.cloned.1.call-update
  153.7 48.3 %reduce-scatter.2.cloned.1.call-done = bf16[4,2,128,256]{3,2,1,0:T(8,128)(2,1)} async-done(((bf16[4,2,1024,256]{3,2,1,0:T(8,128)(2,1)}), bf16[4,2,128,256]{3,2,1,0:T(8,128)(2,1)}) %reduce-scatter.2.cloned.1.call-update) | async-done | bytes 524304 | tf_op jit(solution)/shard_map/reduce_scatter | solution.py:327
  202.0 3.6 %all-to-all-start.2 = ((bf16[4,2,128,256]{3,2,1,0:T(8,128)(2,1)}), bf16[4,2,128,256]{3,2,1,0:T(8,128)(2,1)S(1)}, u32[]{:S(2)}, u32[]{:S(2)}) async-start(bf16[4,2,128,256]{3,2,1,0:T(8,128)(2,1)} %reduce-scatter.2.cloned.1.call-done), calls=%async_computation.3 | async-start | bytes 1048576 | tf_op jit(solution)/shard_map/all_to_all | solution.py:328
  205.6 0.0 copy-start.2
  205.7 0.6 multiply_reduce_fusion
  206.3 5.9 %all-to-all-done.2 = bf16[4,2,128,256]{3,2,1,0:T(8,128)(2,1)S(1)} async-done(((bf16[4,2,128,256]{3,2,1,0:T(8,128)(2,1)}), bf16[4,2,128,256]{3,2,1,0:T(8,128)(2,1)S(1)}, u32[]{:S(2)}, u32[]{:S(2)}) %all-to-all-start.2) | async-done | bytes 524320 | tf_op jit(solution)/shard_map/all_to_all | solution.py:328
  212.2 0.1 convert_bitcast_fusion
  212.3 0.1 copy.21
  212.4 0.7 add_divide_fusion
  213.1 1.8 copy.25
  214.9 1.8 copy.24
  216.7 1.8 copy.23
  (17 shorter events, 0.1 us)
Async XLA Ops:
  7.2 15.0 %copy-start.3 = (f32[1,4096]{1,0:T(1,128)S(1)}, f32[1,4096]{1,0:T(1,128)}, u32[]{:S(2)}) copy-start(f32[1,4096]{1,0:T(1,128)} %param.12) | copy-start | bytes 49156
  7.2 18.9 %copy-start.5 = (s32[4]{0:T(128)S(1)}, s32[4]{0:T(128)}, u32[]{:S(2)}) copy-start(s32[4]{0:T(128)} %param.11) | copy-start | bytes 52
  7.2 19.1 %copy-start.4 = (s32[4]{0:T(128)S(1)}, s32[4]{0:T(128)}, u32[]{:S(2)}) copy-start(s32[4]{0:T(128)} %param.10) | copy-start | bytes 52
  7.2 62.0 %all-gather.2.cloned.1.call-start = ((), (), s32[]{:S(2)}) async-start(), calls=%async_computation.4 | async-start | bytes 4718592 | tf_op jit(solution)/shard_map/all_gather | solution.py:312
  22.8 19.6 %all-to-all-start = ((f32[4,1,1024]{2,1,0:T(1,128)}), f32[4,1,1024]{2,1,0:T(1,128)S(1)}, u32[]{:S(2)}, u32[]{:S(2)}) async-start(f32[4,1,1024]{2,1,0:T(1,128)} %bitcast.2), calls=%async_computation | async-start | bytes 32768 | tf_op jit(solution)/shard_map/all_to_all | solution.py:314
  26.1 175.9 %reduce-scatter.2.cloned.1.call-start = ((), (), s32[]{:S(2)}) async-start(), calls=%async_computation.5 | async-start | bytes 4718592 | tf_op jit(solution)/shard_map/reduce_scatter | solution.py:327
  151.7 1.9 copy-start
  202.0 10.2 %all-to-all-start.2 = ((bf16[4,2,128,256]{3,2,1,0:T(8,128)(2,1)}), bf16[4,2,128,256]{3,2,1,0:T(8,128)(2,1)S(1)}, u32[]{:S(2)}, u32[]{:S(2)}) async-start(bf16[4,2,128,256]{3,2,1,0:T(8,128)(2,1)} %reduce-scatter.2.cloned.1.call-done), calls=%async_computation.3 | async-start | bytes 1048576 | tf_op jit(solution)/shard_map/all_to_all | solution.py:328
  205.6 6.8 %copy-start.1 = (f32[1,512,2,256]{3,2,1,0:T(2,128)S(1)}, f32[1,512,2,256]{3,2,1,0:T(2,128)}, u32[]{:S(2)}) copy-start(f32[1,512,2,256]{3,2,1,0:T(2,128)} %param.15) | copy-start | bytes 3145732
  205.6 6.8 %copy-start.2 = (f32[1,512,2,256]{3,2,1,0:T(2,128)S(1)}, f32[1,512,2,256]{3,2,1,0:T(2,128)}, u32[]{:S(2)}) copy-start(f32[1,512,2,256]{3,2,1,0:T(2,128)} %param.14) | copy-start | bytes 3145732
Sparse Core Ops, SparseCore 0:
  22.3 46.8 all-gather.1
  153.8 48.1 reduce-scatter.1

commit v3 on v2

--- a/solution.py
+++ b/solution.py
@@ -49,14 +49,17 @@
 def chain_kernel(
     sections,
     model_width,
+    load_width,
     tokens_ref,
     cotangent_ref,
-    gains_ref,
+    own_gains_ref,
     owners_ref,
     owners_row_ref,
-    low_ref,
+    rows_ref,
     gradient_ref,
     norm_ref,
+    low,
+    gains,
     hidden,
     scaled,
     grad_out,
@@ -69,12 +72,38 @@
     landed,
     joint,
     squares,
+    terms,
+    sibling_terms,
+    chip_sums,
+    chip_landed,
+    final_out,
+    final_landed,
     send_sem,
     recv_sem,
+    load_sem,
+    rows_send,
+    rows_recv,
+    gains_send,
+    gains_recv,
+    along_send,
+    along_recv,
+    sibling_send,
+    sibling_recv,
+    pair_send,
+    pair_recv,
+    chip_send,
+    chip_recv,
+    final_send,
+    final_recv,
 ):
     me = lax.axis_index("section")
-    tok_rows, held = tokens_ref.shape
+    place = lax.axis_index("dp")
+    chips = lax.axis_size("dp") // 2
+    chip, core = place // 2, lax.rem(place, 2)
+    sibling = chip * 2 + 1 - core
+    _, tok_rows, held = hidden.shape
     width = active.shape[2]
+    part = rows_ref.shape[2]
     block = tok_rows // sections
     own = pl.ds(pl.multiple_of(me * block, block), block)
     peers = [lax.rem(me + d, sections) for d in range(1, sections)]
@@ -84,7 +113,87 @@
         pl.semaphore_signal(
             barrier, inc=1, device_id={"section": peer}, device_id_type=pl.DeviceIdType.MESH
         )
-    pl.semaphore_wait(barrier, sections - 1)
+    ahead = [lax.rem(chip + d, chips) for d in range(1, chips)]
+    behind = [lax.rem(chip + chips - d, chips) for d in range(1, chips)]
+    for other in [sibling] + [a * 2 + core for a in ahead]:
+        pl.semaphore_signal(
+            barrier, inc=1, device_id={"dp": other}, device_id_type=pl.DeviceIdType.MESH
+        )
+    pl.semaphore_wait(barrier, sections - 1 + chips)
+
+    def remote(source, target, sent, received, axis, index):
+        return pltpu.make_async_remote_copy(
+            src_ref=source,
+            dst_ref=target,
+            send_sem=sent,
+            recv_sem=received,
+            device_id={axis: index},
+            device_id_type=pl.DeviceIdType.MESH,
+        )
+
+    def shard(s, at_chip, at_core):
+        row = pl.multiple_of((at_chip * 2 + at_core) * part, part)
+        return low.at[s, :, pl.ds(row, part)]
+
+    pieces = held // load_width
+    loads = []
+    for which, (source, target) in enumerate(
+        ((tokens_ref, hidden.at[0]), (cotangent_ref, grad_out.at[sections - 1]))
+    ):
+        for piece in range(pieces):
+            first = (piece * sections + me) * load_width if pieces > 1 else 0
+            loads.append(
+                pltpu.make_async_copy(
+                    source.at[:, pl.ds(pl.multiple_of(first, load_width), load_width)],
+                    target.at[:, pl.ds(piece * load_width, load_width)],
+                    load_sem.at[which, piece],
+                )
+            )
+
+    def rows_copy(target, slot, source):
+        return remote(
+            rows_ref.at[target], shard(me, chip, core), rows_send.at[slot], rows_recv.at[source],
+            "section", target,
+        )
+
+    def gains_copy(target, slot, source):
+        return remote(
+            own_gains_ref.at[target], gains.at[me], gains_send.at[slot], gains_recv.at[source],
+            "section", target,
+        )
+
+    def along_copy(s, d):
+        return remote(
+            shard(s, chip, core), shard(s, chip, core), along_send.at[s, d], along_recv.at[s, d],
+            "dp", ahead[d] * 2 + core,
+        )
+
+    def sibling_copy(s, slot, at_chip):
+        return remote(
+            shard(s, at_chip, core), shard(s, at_chip, core),
+            sibling_send.at[s, slot], sibling_recv.at[s, slot], "dp", sibling,
+        )
+
+    for d in range(sections - 1):
+        rows_copy(peers[d], d, me).start()
+        gains_copy(peers[d], d, me).start()
+    for load in loads:
+        load.start()
+    low[me, :, pl.ds(pl.multiple_of(place * part, part), part)] = rows_ref[me]
+    gains[me] = own_gains_ref[me]
+
+    def spread_rows(s, carry):
+        @pl.when(s != me)
+        def _():
+            rows_copy(peers[0], 0, s).wait_recv()
+            gains_copy(peers[0], 0, s).wait_recv()
+
+        sibling_copy(s, 0, chip).start()
+        for d in range(chips - 1):
+            along_copy(s, d).start()
+        return carry
+
+    lax.fori_loop(0, sections, spread_rows, 0)
 
     def copies(make, slot):
         return [
@@ -121,14 +230,26 @@
         for copy in sent:
             copy.wait_recv()
 
-    hidden[0] = tokens_ref[...]
     joint[...] = jnp.zeros_like(joint)
+    for load in loads:
+        load.wait()
+    usable = owners_ref[:, :1]
+    for user in range(1, USERS_DEV):
+        usable = usable + owners_ref[:, user : user + 1]
+    grad_out[sections - 1] = (grad_out[sections - 1].astype(jnp.float32) * usable).astype(
+        jnp.bfloat16
+    )
 
     def forward(s, carry):
+        for d in range(chips - 1):
+            along_copy(s, d).wait_recv()
+            sibling_copy(s, d + 1, behind[d]).start()
+        for slot in range(chips):
+            sibling_copy(s, slot, chip).wait_recv()
         widened = hidden[s].astype(jnp.float32)
-        now = (widened * gains_ref[s]).astype(jnp.bfloat16)
+        now = (widened * gains[s]).astype(jnp.bfloat16)
         scaled[s] = now
-        product = jnp.dot(now, low_ref[s, 0], preferred_element_type=jnp.float32)
+        product = jnp.dot(now, low[s, 0], preferred_element_type=jnp.float32)
         square = jnp.sum(widened * widened, axis=-1, keepdims=True)
         own_part[:, :width] = product
         own_part[:, width:] = jnp.broadcast_to(square, (tok_rows, LANES))
@@ -154,18 +275,17 @@
 
         @pl.when(s < sections - 1)
         def _():
-            branch = dot_nt(active[s], low_ref[s, 1])
+            branch = dot_nt(active[s], low[s, 1])
             hidden[s + 1] = (hidden[s].astype(jnp.float32) + branch).astype(jnp.bfloat16)
 
         return carry
 
     lax.fori_loop(0, sections, forward, 0)
-    grad_out[sections - 1] = cotangent_ref[...]
 
     def backward(back, carry):
         s = sections - 1 - back
         step = sections + back
-        product = jnp.dot(grad_out[s], low_ref[s, 1], preferred_element_type=jnp.float32)
+        product = jnp.dot(grad_out[s], low[s, 1], preferred_element_type=jnp.float32)
         own_part[:, :width] = product
         outgoing[step, :, :width] = product.astype(jnp.bfloat16)
         sent = to_owners(step)
@@ -195,7 +315,7 @@
         def _():
             grad_out[s - 1] = (
                 grad_out[s].astype(jnp.float32)
-                + gains_ref[s] * dot_nt(low_grad, low_ref[s, 0])
+                + gains[s] * dot_nt(low_grad, low[s, 0])
                 - hidden[s].astype(jnp.float32) * joined_lanes(whole, width)
             ).astype(jnp.bfloat16)
 
@@ -225,16 +345,106 @@
     for user in range(1, USERS_DEV):
         token_factor = token_factor + owners_ref[:, user : user + 1] * factors[user : user + 1, :1]
 
-    def products(s, carry):
+    def pair_copy(s):
+        return remote(
+            terms.at[s, 1 - core], sibling_terms.at[s], pair_send.at[s], pair_recv.at[s],
+            "dp", sibling,
+        )
+
+    def chip_copy(s, d):
+        return remote(
+            chip_sums.at[s, ahead[d]], chip_landed.at[s, d], chip_send.at[s, d],
+            chip_recv.at[s, d], "dp", ahead[d] * 2 + core,
+        )
+
+    def final_copy(target, source):
+        return remote(
+            final_out.at[target], final_landed.at[me], final_send.at[target],
+            final_recv.at[source], "section", target,
+        )
+
+    def products(s):
         weighted_inner = (grad_scaled[s, :, :width].astype(jnp.float32) * token_factor).astype(
             jnp.bfloat16
         )
         weighted_out = (grad_out[s].astype(jnp.float32) * token_factor).astype(jnp.bfloat16)
-        gradient_ref[s, 0] = dot_tn(scaled[s], weighted_inner).astype(jnp.bfloat16)
-        gradient_ref[s, 1] = dot_tn(weighted_out, active[s]).astype(jnp.bfloat16)
-        return carry
-
-    lax.fori_loop(0, sections, products, 0)
+        down = dot_tn(scaled[s], weighted_inner).astype(jnp.bfloat16)
+        up = dot_tn(weighted_out, active[s]).astype(jnp.bfloat16)
+        for at_chip in range(chips):
+            for at_core in range(2):
+                row = (at_chip * 2 + at_core) * part
+                terms[s, at_core, at_chip, 0] = down[row : row + part]
+                terms[s, at_core, at_chip, 1] = up[row : row + part]
+        pair_copy(s).start()
+
+    def chip_sum(s):
+        pair_copy(s).wait_recv()
+        chip_sums[s] = (
+            terms[s, core].astype(jnp.float32) + sibling_terms[s].astype(jnp.float32)
+        ).astype(jnp.bfloat16)
+        for d in range(chips - 1):
+            chip_copy(s, d).start()
+
+    products(0)
+
+    def products_step(s, carry):
+        products(s)
+        chip_sum(s - 1)
+        return carry
+
+    lax.fori_loop(1, sections, products_step, 0)
+    chip_sum(sections - 1)
+
+    def finish(s, carry):
+        total = terms[s, core, chip].astype(jnp.float32) + sibling_terms[s, chip].astype(
+            jnp.float32
+        )
+        for d in range(chips - 1):
+            chip_copy(s, d).wait_recv()
+            total = total + chip_landed[s, d].astype(jnp.float32)
+        final_out[s] = total.astype(jnp.bfloat16)
+
+        @pl.when(s != me)
+        def _():
+            final_copy(s, me).start()
+
+        @pl.when(s == me)
+        def _():
+            final_landed[s] = final_out[s]
+
+        return carry
+
+    lax.fori_loop(0, sections, finish, 0)
+
+    def collect(s, carry):
+        @pl.when(s != me)
+        def _():
+            final_copy(s, s).wait_recv()
+
+        gradient_ref[s] = final_landed[s]
+        return carry
+
+    lax.fori_loop(0, sections, collect, 0)
+
+    for d in range(sections - 1):
+        rows_copy(peers[d], d, me).wait_send()
+        gains_copy(peers[d], d, me).wait_send()
+
+    def drain_rows(s, carry):
+        for slot in range(chips):
+            sibling_copy(s, slot, chip).wait_send()
+        for d in range(chips - 1):
+            along_copy(s, d).wait_send()
+            chip_copy(s, d).wait_send()
+        pair_copy(s).wait_send()
+
+        @pl.when(s != me)
+        def _():
+            final_copy(s, me).wait_send()
+
+        return carry
+
+    lax.fori_loop(0, sections, drain_rows, 0)
 
     def drain(step, carry):
         for copy in to_owners(step) + to_all(active, 0, step):
@@ -252,25 +462,31 @@
         copy.wait_send()
 
 
-def chain(tokens, cotangent, gains, owners, low, model_width):
-    sections, _, held, width = low.shape
+def chain(tokens, cotangent, gains, owners, rows, shards, load_width, model_width):
+    sections, _, part, width = rows.shape
+    held = part * shards
     tok_rows = tokens.shape[0]
     block = tok_rows // sections
+    chips = shards // 2
     vmem = pl.BlockSpec(memory_space=pltpu.VMEM)
+    anywhere = pl.BlockSpec(memory_space=pl.ANY)
     owners_row = jnp.pad(owners.T, ((0, 8 - USERS_DEV), (0, 0)))
     owners = jnp.pad(owners, ((0, 0), (0, LANES - USERS_DEV)))
     steps = 2 * sections
     copies = (2 * steps + 1, sections - 1)
     bf16, f32 = jnp.bfloat16, jnp.float32
+    dma = pltpu.SemaphoreType.DMA
     return pl.pallas_call(
-        functools.partial(chain_kernel, sections, model_width),
+        functools.partial(chain_kernel, sections, model_width, load_width),
         out_shape=(
-            jax.ShapeDtypeStruct(low.shape, bf16),
+            jax.ShapeDtypeStruct(rows.shape, bf16),
             jax.ShapeDtypeStruct((8, LANES), f32),
         ),
-        in_specs=[vmem] * 6,
+        in_specs=[anywhere, anywhere, vmem, vmem, vmem, vmem],
         out_specs=(vmem, vmem),
         scratch_shapes=[
+            pltpu.VMEM((sections, 2, held, width), bf16),
+            pltpu.VMEM((sections, 1, held), f32),
             pltpu.VMEM((sections, tok_rows, held), bf16),
             pltpu.VMEM((sections, tok_rows, held), bf16),
             pltpu.VMEM((sections, tok_rows, held), bf16),
@@ -283,13 +499,34 @@
             pltpu.VMEM((steps, sections - 1, block, width + LANES), bf16),
             pltpu.VMEM((tok_rows, tok_rows), f32),
             pltpu.VMEM((sections, 8, LANES), f32),
-            pltpu.SemaphoreType.DMA(copies),
-            pltpu.SemaphoreType.DMA(copies),
+            pltpu.VMEM((sections, 2, chips, 2, part, width), bf16),
+            pltpu.VMEM((sections, chips, 2, part, width), bf16),
+            pltpu.VMEM((sections, chips, 2, part, width), bf16),
+            pltpu.VMEM((sections, chips - 1, 2, part, width), bf16),
+            pltpu.VMEM((sections, 2, part, width), bf16),
+            pltpu.VMEM((sections, 2, part, width), bf16),
+            dma(copies),
+            dma(copies),
+            dma((2, held // load_width)),
+            dma((sections - 1,)),
+            dma((sections,)),
+            dma((sections - 1,)),
+            dma((sections,)),
+            dma((sections, chips - 1)),
+            dma((sections, chips - 1)),
+            dma((sections, chips)),
+            dma((sections, chips)),
+            dma((sections,)),
+            dma((sections,)),
+            dma((sections, chips - 1)),
+            dma((sections, chips - 1)),
+            dma((sections,)),
+            dma((sections,)),
         ],
         compiler_params=pltpu.CompilerParams(
-            collective_id=0, has_side_effects=True, vmem_limit_bytes=48 * 1024 * 1024
+            collective_id=0, has_side_effects=True, vmem_limit_bytes=52 * 1024 * 1024
         ),
-    )(tokens, cotangent, gains[:, None, :], owners, owners_row, low)
+    )(tokens, cotangent, gains, owners, owners_row, rows)
 
 
 def on_device(
@@ -308,10 +545,9 @@
         return lax.dynamic_index_in_dim(split, quarter, 2, keepdims=False).reshape(tok_rows, held)
 
     low = weights[0].astype(jnp.bfloat16).reshape(sections, part, 2, width)
-    low = lax.all_to_all(low.transpose(0, 2, 1, 3), "section", 0, 0, tiled=True)
-    low = lax.all_gather(low, "dp", axis=2, tiled=True)
+    low = low.transpose(0, 2, 1, 3)
     gains = norm_gains[0].reshape(shards, sections, part).transpose(1, 0, 2)
-    gains = lax.all_to_all(gains.reshape(sections, held), "section", 0, 0, tiled=True)
+    gains = gains.reshape(sections, 1, held)
 
     positions = jnp.arange(tok_rows) % SEQLEN
     usable = positions < jnp.repeat(lengths, SEQLEN)
@@ -321,11 +557,13 @@
         jnp.float32
     )
 
-    seeds = own_features(cotangent) * usable[:, None].astype(jnp.bfloat16)
-    gradient, norms = chain(own_features(tokens), seeds, gains, owners, low, model_width)
+    load_width = part
+    if part % LANES != 0:
+        tokens, cotangent, load_width = own_features(tokens), own_features(cotangent), held
+    gradient, norms = chain(
+        tokens, cotangent, gains, owners, low, shards, load_width, model_width
+    )
     user_norm = norms[:USERS_DEV, 0]
-    gradient = lax.psum_scatter(gradient, "dp", scatter_dimension=2, tiled=True)
-    gradient = lax.all_to_all(gradient, "section", 0, 0, tiled=True)
     gradient = gradient.transpose(0, 2, 1, 3).reshape(own_rows, 2, width).astype(jnp.float32)
     moment_one = BETA_ONE * first_moment[0] + (1.0 - BETA_ONE) * gradient
     moment_two = BETA_TWO * second_moment[0] + (1.0 - BETA_TWO) * gradient * gradient

time: 226 us -> 182 us (0.81)
  the two profiles are of different devices: /device:TPU:0 before, /device:TPU:30 now
where the time goes in v3:
time: 182 us
  Pallas kernels  170 us (93%)
  local copies, waits for them, and re-layouts  9.15 us (5%)
  other arithmetic  2.23 us (1%)
    pallas_call x1, Pallas kernels, chain(): pl.pallas_call(functools.partial(chain_kernel, sections, model_width, loa...  170 us
    unnamed x8, local copies, waits for them, and re-layouts  7.33 us

profile of v3, /device:TPU:30, one launch (start us, length us, event | category | flops | bytes accessed | tf_op | source)
XLA Modules:
  0.0 182.1 jit_solution(3190803586094888628)
XLA Ops:
  0.6 0.7 broadcast_subtract_fusion
  1.3 0.1 broadcast_in_dim.4
  1.4 0.1 eq.24
  1.5 0.7 broadcast_in_dim.5
  2.2 0.1 reshape.62
  2.3 0.7 copy.14
  3.0 0.1 fusion.2
  3.2 1.3 copy.30
  4.5 170.0 %shard_map.111 = (bf16[4,2,128,256]{3,2,1,0:T(8,128)(2,1)S(1)}, f32[8,128]{1,0:T(8,128)S(1)}) custom-call(bf16[256,4096]{1,0:T(8,128)(2,1)} %tokens_ref.1, bf16[256,4096]{1,0:T(8,128)(2,1)} %cotangent_ref.1, f32[4,1,1024]{2,1,0:T(1,128)S(1)} %bitcast.18, f32[256,128]{1,0:T(8,128)S(1)} %pad_convert_fusion.owners_ref, ...), custom_call_target="tpu_custom_call" | custom-call | tf_op jit(solution)/shard_map/pallas_call | solution.py:479
  174.5 0.0 copy-start
  174.5 0.0 copy-start.1
  174.5 0.6 multiply_reduce_fusion
  175.1 0.1 convert_bitcast_fusion
  175.2 0.1 copy.17
  175.3 0.4 copy-done
  175.7 0.3 copy-done.1
  176.0 0.7 add_divide_fusion
  176.7 1.8 copy.21
  178.5 1.8 copy.20
  180.3 1.8 copy.19
  (5 shorter events, 0.1 us)
Async XLA Ops:
  174.5 1.2 copy-start
  174.5 1.5 copy-start.1

commit v4 on v3

--- a/solution.py
+++ b/solution.py
@@ -78,6 +78,8 @@
     chip_landed,
     final_out,
     final_landed,
+    relay_landed,
+    total_ref,
     send_sem,
     recv_sem,
     load_sem,
@@ -95,6 +97,9 @@
     chip_recv,
     final_send,
     final_recv,
+    onward_send,
+    relay_send,
+    relay_recv,
 ):
     me = lax.axis_index("section")
     place = lax.axis_index("dp")
@@ -182,7 +187,28 @@
     low[me, :, pl.ds(pl.multiple_of(place * part, part), part)] = rows_ref[me]
     gains[me] = own_gains_ref[me]
 
-    def spread_rows(s, carry):
+    last = chips - 1
+    relayed = chips >= 4
+
+    def when_not(excluded, run):
+        if not excluded:
+            run()
+            return
+        allowed = chip != excluded[0]
+        for other in excluded[1:]:
+            allowed = allowed & (chip != other)
+        pl.when(allowed)(run)
+
+    def not_sent(d):
+        return [c for c, at in ((0, chips - 2), (last, 0)) if relayed and d == at]
+
+    def held_back(d):
+        return [c for c, at in ((1, chips - 3), (last - 1, 1)) if relayed and d == at]
+
+    def not_received(d):
+        return [c for c, at in ((last, chips - 2), (0, 0)) if relayed and d == at]
+
+    def spread_rows(s):
         @pl.when(s != me)
         def _():
             rows_copy(peers[0], 0, s).wait_recv()
@@ -190,10 +216,27 @@
 
         sibling_copy(s, 0, chip).start()
         for d in range(chips - 1):
-            along_copy(s, d).start()
-        return carry
-
-    lax.fori_loop(0, sections, spread_rows, 0)
+            when_not(not_sent(d), along_copy(s, d).start)
+
+    def rows_left(s):
+        for d in range(chips - 1):
+            when_not(not_sent(d), along_copy(s, d).wait_send)
+
+    def onward_high(s):
+        return remote(
+            shard(s, 0, core), shard(s, 0, core), onward_send.at[s],
+            along_recv.at[s, chips - 2], "dp", last * 2 + core,
+        )
+
+    def onward_low(s):
+        return remote(
+            shard(s, last, core), shard(s, last, core), onward_send.at[s],
+            along_recv.at[s, 0], "dp", core,
+        )
+
+    spread_rows(0)
+    rows_left(0)
+    spread_rows(1)
 
     def copies(make, slot):
         return [
@@ -241,8 +284,12 @@
     )
 
     def forward(s, carry):
-        for d in range(chips - 1):
+        for d in [*range(1, chips - 2), 0, chips - 2] if relayed else range(chips - 1):
             along_copy(s, d).wait_recv()
+            if relayed and d == chips - 3:
+                pl.when(chip == last - 1)(onward_high(s).start)
+            if relayed and d == 1:
+                pl.when(chip == 1)(onward_low(s).start)
             sibling_copy(s, d + 1, behind[d]).start()
         for slot in range(chips):
             sibling_copy(s, slot, chip).wait_recv()
@@ -257,6 +304,12 @@
         outgoing[s, :, width:] = split_lanes(square, tok_rows)
         sent = to_owners(s)
         start(sent)
+
+        @pl.when(s + 2 < sections)
+        def _():
+            rows_left(s + 1)
+            spread_rows(s + 2)
+
         arrived(sent)
         total = own_part[own, :width]
         mean = own_part[own, width : width + 1]
@@ -383,26 +436,70 @@
             terms[s, core].astype(jnp.float32) + sibling_terms[s].astype(jnp.float32)
         ).astype(jnp.bfloat16)
         for d in range(chips - 1):
-            chip_copy(s, d).start()
+            when_not(not_sent(d) + held_back(d), chip_copy(s, d).start)
+        if relayed:
+            pl.when(chip == 0)(from_low(s).start)
+            pl.when(chip == last)(from_high(s).start)
+
+    def from_low(s):
+        return remote(
+            chip_sums.at[s, last], relay_landed.at[s], relay_send.at[s], relay_recv.at[s],
+            "dp", 2 + core,
+        )
+
+    def from_high(s):
+        return remote(
+            chip_sums.at[s, 0], relay_landed.at[s], relay_send.at[s], relay_recv.at[s],
+            "dp", (last - 1) * 2 + core,
+        )
+
+    def add_relayed(s, target):
+        from_low(s).wait_recv()
+        chip_sums[s, target] = (
+            chip_sums[s, target].astype(jnp.float32) + relay_landed[s].astype(jnp.float32)
+        ).astype(jnp.bfloat16)
+
+    def relay_sum(s):
+        if not relayed:
+            return
+
+        @pl.when(chip == 1)
+        def _():
+            add_relayed(s, last)
+            chip_copy(s, chips - 3).start()
+
+        @pl.when(chip == last - 1)
+        def _():
+            add_relayed(s, 0)
+            chip_copy(s, 1).start()
 
     products(0)
+    products(1)
+    chip_sum(0)
 
     def products_step(s, carry):
         products(s)
         chip_sum(s - 1)
+        relay_sum(s - 2)
         return carry
 
-    lax.fori_loop(1, sections, products_step, 0)
+    lax.fori_loop(2, sections, products_step, 0)
     chip_sum(sections - 1)
+    relay_sum(sections - 2)
+    relay_sum(sections - 1)
 
     def finish(s, carry):
-        total = terms[s, core, chip].astype(jnp.float32) + sibling_terms[s, chip].astype(
-            jnp.float32
-        )
+        total_ref[...] = terms[s, core, chip].astype(jnp.float32) + sibling_terms[
+            s, chip
+        ].astype(jnp.float32)
         for d in range(chips - 1):
-            chip_copy(s, d).wait_recv()
-            total = total + chip_landed[s, d].astype(jnp.float32)
-        final_out[s] = total.astype(jnp.bfloat16)
+
+            def add(d=d):
+                chip_copy(s, d).wait_recv()
+                total_ref[...] += chip_landed[s, d].astype(jnp.float32)
+
+            when_not(not_received(d), add)
+        final_out[s] = total_ref[...].astype(jnp.bfloat16)
 
         @pl.when(s != me)
         def _():
@@ -434,8 +531,10 @@
         for slot in range(chips):
             sibling_copy(s, slot, chip).wait_send()
         for d in range(chips - 1):
-            along_copy(s, d).wait_send()
-            chip_copy(s, d).wait_send()
+            when_not(not_sent(d), chip_copy(s, d).wait_send)
+        if relayed:
+            pl.when((chip == 1) | (chip == last - 1))(onward_high(s).wait_send)
+            pl.when((chip == 0) | (chip == last))(from_low(s).wait_send)
         pair_copy(s).wait_send()
 
         @pl.when(s != me)
@@ -444,6 +543,7 @@
 
         return carry
 
+    rows_left(sections - 1)
     lax.fori_loop(0, sections, drain_rows, 0)
 
     def drain(step, carry):
@@ -505,6 +605,8 @@
             pltpu.VMEM((sections, chips - 1, 2, part, width), bf16),
             pltpu.VMEM((sections, 2, part, width), bf16),
             pltpu.VMEM((sections, 2, part, width), bf16),
+            pltpu.VMEM((sections, 2, part, width), bf16),
+            pltpu.VMEM((2, part, width), f32),
             dma(copies),
             dma(copies),
             dma((2, held // load_width)),
@@ -520,6 +622,9 @@
             dma((sections,)),
             dma((sections, chips - 1)),
             dma((sections, chips - 1)),
+            dma((sections,)),
+            dma((sections,)),
+            dma((sections,)),
             dma((sections,)),
             dma((sections,)),
         ],

time: 182 us -> 179 us (0.984)
  the two profiles are of different devices: /device:TPU:30 before, /device:TPU:0 now
where the time goes in v4:
time: 179 us; the launch traced here: 177 us
  Pallas kernels  165 us (92%)
  local copies, waits for them, and re-layouts  9.15 us (5%)
  other arithmetic  2.23 us (1%)
    pallas_call x1, Pallas kernels, chain(): pl.pallas_call(functools.partial(chain_kernel, sections, model_width, loa...  165 us
    unnamed x8, local copies, waits for them, and re-layouts  7.33 us

profile of v4, /device:TPU:0, one launch (start us, length us, event | category | flops | bytes accessed | tf_op | source)
XLA Modules:
  0.0 176.7 jit_solution(14707384827670109613)
XLA Ops:
  0.6 0.7 broadcast_subtract_fusion
  1.3 0.1 broadcast_in_dim.4
  1.4 0.1 eq.24
  1.5 0.7 broadcast_in_dim.5
  2.2 0.1 reshape.62
  2.3 0.7 copy.14
  3.0 0.1 fusion.2
  3.2 1.3 copy.30
  4.5 164.6 %shard_map.111 = (bf16[4,2,128,256]{3,2,1,0:T(8,128)(2,1)S(1)}, f32[8,128]{1,0:T(8,128)S(1)}) custom-call(bf16[256,4096]{1,0:T(8,128)(2,1)} %tokens_ref.1, bf16[256,4096]{1,0:T(8,128)(2,1)} %cotangent_ref.1, f32[4,1,1024]{2,1,0:T(1,128)S(1)} %bitcast.18, f32[256,128]{1,0:T(8,128)S(1)} %pad_convert_fusion.owners_ref, ...), custom_call_target="tpu_custom_call" | custom-call | tf_op jit(solution)/shard_map/pallas_call | solution.py:579
  169.2 0.0 copy-start
  169.2 0.0 copy-start.1
  169.2 0.6 multiply_reduce_fusion
  169.8 0.1 convert_bitcast_fusion
  169.9 0.1 copy.17
  170.0 0.4 copy-done
  170.4 0.3 copy-done.1
  170.7 0.7 add_divide_fusion
  171.4 1.8 %copy.21 = f32[1,512,2,256]{3,2,1,0:T(2,128)} copy(f32[1,512,2,256]{3,1,2,0:T(8,128)S(1)} %get-tuple-element.12) | data formatting | bytes 2097152
  173.2 1.8 %copy.20 = f32[1,512,2,256]{3,2,1,0:T(2,128)} copy(f32[1,512,2,256]{3,1,2,0:T(8,128)S(1)} %get-tuple-element.13) | data formatting | bytes 2097152
  174.9 1.8 %copy.19 = f32[1,512,2,256]{3,2,1,0:T(2,128)} copy(f32[1,512,2,256]{3,1,2,0:T(8,128)S(1)} %get-tuple-element.14) | data formatting | bytes 2097152
  (5 shorter events, 0.1 us)
Async XLA Ops:
  169.2 1.2 copy-start
  169.2 1.5 copy-start.1

commit v5 on v4

--- a/solution.py
+++ b/solution.py
@@ -4,6 +4,7 @@
 import jax.numpy as jnp
 from jax import lax
 from jax.experimental import pallas as pl
+from jax.experimental.layout import Layout, with_layout_constraint
 from jax.experimental.pallas import tpu as pltpu
 from jax.sharding import PartitionSpec as P
 
@@ -20,6 +21,7 @@
 ADAM_EPS = 1e-08
 NORM_EPS = 1e-05
 LANES = 128
+HALVES = 2
 
 
 def dot_nt(left, right):
@@ -109,8 +111,10 @@
     _, tok_rows, held = hidden.shape
     width = active.shape[2]
     part = rows_ref.shape[2]
-    block = tok_rows // sections
-    own = pl.ds(pl.multiple_of(me * block, block), block)
+    half = tok_rows // HALVES
+    block = half // sections
+    whole = [pl.ds(h * half, half) for h in range(HALVES)]
+    mine = [pl.ds(h * block, block) for h in range(HALVES)]
     peers = [lax.rem(me + d, sections) for d in range(1, sections)]
 
     barrier = pltpu.get_barrier_semaphore()
@@ -252,18 +256,20 @@
             for source, target in [make(d)]
         ]
 
-    def to_owners(step):
+    def block_of(h, index):
+        return pl.ds(pl.multiple_of(h * half + index * block, block), block)
+
+    def to_owners(step, h):
         def make(d):
-            rows = pl.ds(pl.multiple_of(peers[d] * block, block), block)
-            return outgoing.at[step, rows], landed.at[step, d]
-
-        return copies(make, 2 * step)
-
-    def to_all(ref, s, step):
+            return outgoing.at[step, block_of(h, peers[d])], landed.at[step, d, mine[h]]
+
+        return copies(make, 2 * step * HALVES + h)
+
+    def to_all(ref, s, step, h):
         def make(d):
-            return ref.at[s, own], ref.at[s, own]
-
-        return copies(make, 2 * step + 1)
+            return ref.at[s, block_of(h, me)], ref.at[s, block_of(h, me)]
+
+        return copies(make, (2 * step + 1) * HALVES + h)
 
     def start(sent):
         for copy in sent:
@@ -293,89 +299,105 @@
             sibling_copy(s, d + 1, behind[d]).start()
         for slot in range(chips):
             sibling_copy(s, slot, chip).wait_recv()
-        widened = hidden[s].astype(jnp.float32)
-        now = (widened * gains[s]).astype(jnp.bfloat16)
-        scaled[s] = now
-        product = jnp.dot(now, low[s, 0], preferred_element_type=jnp.float32)
-        square = jnp.sum(widened * widened, axis=-1, keepdims=True)
-        own_part[:, :width] = product
-        own_part[:, width:] = jnp.broadcast_to(square, (tok_rows, LANES))
-        outgoing[s, :, :width] = product.astype(jnp.bfloat16)
-        outgoing[s, :, width:] = split_lanes(square, tok_rows)
-        sent = to_owners(s)
-        start(sent)
+        for h in range(HALVES):
+
+            @pl.when(s > 0)
+            def _():
+                arrived(to_all(active, s - 1, s - 1, h))
+                branch = dot_nt(active[s - 1, whole[h]], low[s - 1, 1])
+                hidden[s, whole[h]] = (
+                    hidden[s - 1, whole[h]].astype(jnp.float32) + branch
+                ).astype(jnp.bfloat16)
+
+            widened = hidden[s, whole[h]].astype(jnp.float32)
+            now = (widened * gains[s]).astype(jnp.bfloat16)
+            scaled[s, whole[h]] = now
+            product = jnp.dot(now, low[s, 0], preferred_element_type=jnp.float32)
+            square = jnp.sum(widened * widened, axis=-1, keepdims=True)
+            own_part[whole[h], :width] = product
+            own_part[whole[h], width:] = jnp.broadcast_to(square, (half, LANES))
+            outgoing[s, whole[h], :width] = product.astype(jnp.bfloat16)
+            outgoing[s, whole[h], width:] = split_lanes(square, half)
+            start(to_owners(s, h))
 
         @pl.when(s + 2 < sections)
         def _():
             rows_left(s + 1)
             spread_rows(s + 2)
 
-        arrived(sent)
-        total = own_part[own, :width]
-        mean = own_part[own, width : width + 1]
-        for d in range(sections - 1):
-            piece = landed[s, d]
-            total = total + piece[:, :width].astype(jnp.float32)
-            mean = mean + joined_lanes(piece, width)
-        scale = lax.rsqrt(mean / model_width + NORM_EPS)
-        value = total * scale
-        inner[s] = value
-        inverse[s] = jnp.broadcast_to(scale, (block, LANES))
-        active[s, own] = (value / (1.0 + jnp.exp(-value))).astype(jnp.bfloat16)
-        sent = to_all(active, s, s)
-        start(sent)
-        arrived(sent)
-
-        @pl.when(s < sections - 1)
-        def _():
-            branch = dot_nt(active[s], low[s, 1])
-            hidden[s + 1] = (hidden[s].astype(jnp.float32) + branch).astype(jnp.bfloat16)
-
+        for h in range(HALVES):
+            arrived(to_owners(s, h))
+            total = own_part[block_of(h, me), :width]
+            mean = own_part[block_of(h, me), width : width + 1]
+            for d in range(sections - 1):
+                piece = landed[s, d, mine[h]]
+                total = total + piece[:, :width].astype(jnp.float32)
+                mean = mean + joined_lanes(piece, width)
+            scale = lax.rsqrt(mean / model_width + NORM_EPS)
+            value = total * scale
+            inner[s, mine[h]] = value
+            inverse[s, mine[h]] = jnp.broadcast_to(scale, (block, LANES))
+            active[s, block_of(h, me)] = (value / (1.0 + jnp.exp(-value))).astype(jnp.bfloat16)
+            start(to_all(active, s, s, h))
         return carry
 
     lax.fori_loop(0, sections, forward, 0)
+    for h in range(HALVES):
+        arrived(to_all(active, sections - 1, sections - 1, h))
+
+    def inner_gram(s):
+        low_grad = grad_scaled[s, :, :width]
+        joint[...] += dot_nt(scaled[s], scaled[s]) * dot_nt(low_grad, low_grad)
 
     def backward(back, carry):
         s = sections - 1 - back
         step = sections + back
-        product = jnp.dot(grad_out[s], low[s, 1], preferred_element_type=jnp.float32)
-        own_part[:, :width] = product
-        outgoing[step, :, :width] = product.astype(jnp.bfloat16)
-        sent = to_owners(step)
-        start(sent)
+        for h in range(HALVES):
+
+            @pl.when(back > 0)
+            def _():
+                arrived(to_all(grad_scaled, s + 1, step - 1, h))
+                block_in = grad_scaled[s + 1, whole[h]]
+                grad_out[s, whole[h]] = (
+                    grad_out[s + 1, whole[h]].astype(jnp.float32)
+                    + gains[s + 1] * dot_nt(block_in[:, :width], low[s + 1, 0])
+                    - hidden[s + 1, whole[h]].astype(jnp.float32) * joined_lanes(block_in, width)
+                ).astype(jnp.bfloat16)
+
+            product = jnp.dot(
+                grad_out[s, whole[h]], low[s, 1], preferred_element_type=jnp.float32
+            )
+            own_part[whole[h], :width] = product
+            outgoing[step, whole[h], :width] = product.astype(jnp.bfloat16)
+            start(to_owners(step, h))
+
         joint[...] += dot_nt(active[s], active[s]) * dot_nt(grad_out[s], grad_out[s])
-        arrived(sent)
-        total = own_part[own, :width]
-        for d in range(sections - 1):
-            total = total + landed[step, d, :, :width].astype(jnp.float32)
-        value = inner[s]
-        scale = inverse[s][:, :1]
-        sigmoid_val = 1.0 / (1.0 + jnp.exp(-value))
-        grad_inner = total * sigmoid_val * (1.0 + value * (1.0 - sigmoid_val))
-        pull = jnp.sum(grad_inner * value, axis=-1, keepdims=True) * (
-            scale * scale / model_width
-        )
-        grad_scaled[s, own, :width] = (grad_inner * scale).astype(jnp.bfloat16)
-        grad_scaled[s, own, width:] = split_lanes(pull, block)
-        sent = to_all(grad_scaled, s, step)
-        start(sent)
-        gram = dot_nt(scaled[s], scaled[s])
-        arrived(sent)
-        whole = grad_scaled[s]
-        low_grad = whole[:, :width]
-
-        @pl.when(s > 0)
-        def _():
-            grad_out[s - 1] = (
-                grad_out[s].astype(jnp.float32)
-                + gains[s] * dot_nt(low_grad, low[s, 0])
-                - hidden[s].astype(jnp.float32) * joined_lanes(whole, width)
-            ).astype(jnp.bfloat16)
-
-        joint[...] += gram * dot_nt(low_grad, low_grad)
+        for h in range(HALVES):
+            arrived(to_owners(step, h))
+            total = own_part[block_of(h, me), :width]
+            for d in range(sections - 1):
+                total = total + landed[step, d, mine[h], :width].astype(jnp.float32)
+            value = inner[s, mine[h]]
+            scale = inverse[s, mine[h]][:, :1]
+            sigmoid_val = 1.0 / (1.0 + jnp.exp(-value))
+            grad_inner = total * sigmoid_val * (1.0 + value * (1.0 - sigmoid_val))
+            pull = jnp.sum(grad_inner * value, axis=-1, keepdims=True) * (
+                scale * scale / model_width
+            )
+            grad_scaled[s, block_of(h, me), :width] = (grad_inner * scale).astype(jnp.bfloat16)
+            grad_scaled[s, block_of(h, me), width:] = split_lanes(pull, block)
+            start(to_all(grad_scaled, s, step, h))
+
+        @pl.when(back > 0)
+        def _():
+            inner_gram(s + 1)
+
         return carry
 
     lax.fori_loop(0, sections, backward, 0)
+    for h in range(HALVES):
+        arrived(to_all(grad_scaled, 0, 2 * sections - 1, h))
+    inner_gram(0)
 
     row_of = lax.broadcasted_iota(jnp.int32, (8, LANES), 0)
     sums = jnp.zeros((8, LANES), jnp.float32)
@@ -385,7 +407,7 @@
         whole_sum = jnp.sum(held_sum, axis=0, keepdims=True)
         sums = jnp.where(row_of == user, whole_sum, sums)
     squares[me] = sums
-    sent = copies(lambda d: (squares.at[me], squares.at[me]), 4 * sections)
+    sent = copies(lambda d: (squares.at[me], squares.at[me]), 4 * sections * HALVES)
     start(sent)
     arrived(sent)
     total = squares[0]
@@ -547,13 +569,15 @@
     lax.fori_loop(0, sections, drain_rows, 0)
 
     def drain(step, carry):
-        for copy in to_owners(step) + to_all(active, 0, step):
-            copy.wait_send()
+        for h in range(HALVES):
+            for copy in to_owners(step, h) + to_all(active, 0, step, h):
+                copy.wait_send()
         return carry
 
     def drain_back(step, carry):
-        for copy in to_owners(step) + to_all(grad_scaled, 0, step):
-            copy.wait_send()
+        for h in range(HALVES):
+            for copy in to_owners(step, h) + to_all(grad_scaled, 0, step, h):
+                copy.wait_send()
         return carry
 
     lax.fori_loop(0, sections, drain, 0)
@@ -573,7 +597,7 @@
     owners_row = jnp.pad(owners.T, ((0, 8 - USERS_DEV), (0, 0)))
     owners = jnp.pad(owners, ((0, 0), (0, LANES - USERS_DEV)))
     steps = 2 * sections
-    copies = (2 * steps + 1, sections - 1)
+    copies = (2 * steps * HALVES + 1, sections - 1)
     bf16, f32 = jnp.bfloat16, jnp.float32
     dma = pltpu.SemaphoreType.DMA
     return pl.pallas_call(
@@ -669,7 +693,8 @@
         tokens, cotangent, gains, owners, low, shards, load_width, model_width
     )
     user_norm = norms[:USERS_DEV, 0]
-    gradient = gradient.transpose(0, 2, 1, 3).reshape(own_rows, 2, width).astype(jnp.float32)
+    gradient = gradient.transpose(0, 2, 1, 3).reshape(own_rows, 2, width)
+    gradient = with_layout_constraint(gradient, Layout((0, 1, 2))).astype(jnp.float32)
     moment_one = BETA_ONE * first_moment[0] + (1.0 - BETA_ONE) * gradient
     moment_two = BETA_TWO * second_moment[0] + (1.0 - BETA_TWO) * gradient * gradient
     direction = moment_one / FIRST_FIX / (jnp.sqrt(moment_two / SECOND_FIX) + ADAM_EPS)

time: 179 us -> 166 us (0.927)
  Pallas kernels: 165 us -> 154 us
  local copies, waits for them, and re-layouts: 9.15 us -> 3.56 us
  other arithmetic: 2.23 us -> 5.87 us
    pallas_call x1, Pallas kernels: 165 us -> 154 us  [chain(): pl.pallas_call(functools.partial(chain_kernel, sections, model_width, loa...]
    unnamed x8 -> x5, local copies, waits for them, and re-layouts: 7.33 us -> 1.3 us
    broadcast_in_dim x0 -> x1, other arithmetic: none -> 4.41 us  [on_device(): direction[None]]
where the time goes in v5:
time: 166 us; the launch traced here: 164 us
  Pallas kernels  154 us (93%)
  other arithmetic  5.87 us (4%)
  local copies, waits for them, and re-layouts  3.56 us (2%)
    pallas_call x1, Pallas kernels, chain(): pl.pallas_call(functools.partial(chain_kernel, sections, model_width, loa...  154 us
    broadcast_in_dim x1, other arithmetic, on_device(): direction[None]  4.41 us

profile of v5, /device:TPU:0, one launch (start us, length us, event | category | flops | bytes accessed | tf_op | source)
XLA Modules:
  0.0 163.8 jit_solution(18042623809143263273)
XLA Ops:
  0.6 0.7 broadcast_subtract_fusion
  1.3 0.1 broadcast_in_dim.17
  1.4 0.1 eq.24
  1.5 0.7 broadcast_in_dim.18
  2.2 0.1 reshape.42
  2.3 0.7 copy.14
  3.0 0.1 fusion.3
  3.2 1.3 copy.20
  4.5 0.0 copy-start
  4.5 0.0 copy-start.1
  4.5 153.7 %shard_map.111 = (bf16[4,2,128,256]{3,2,1,0:T(8,128)(2,1)S(1)}, f32[8,128]{1,0:T(8,128)S(1)}) custom-call(bf16[256,4096]{1,0:T(8,128)(2,1)} %tokens_ref.1, bf16[256,4096]{1,0:T(8,128)(2,1)} %cotangent_ref.1, f32[4,1,1024]{2,1,0:T(1,128)S(1)} %bitcast.26, f32[256,128]{1,0:T(8,128)S(1)} %pad_convert_fusion.owners_ref, ...), custom_call_target="tpu_custom_call" | custom-call | tf_op jit(solution)/shard_map/pallas_call | solution.py:603
  158.2 0.5 copy.17
  158.8 0.6 multiply_reduce_fusion
  159.4 0.0 copy-done
  159.4 0.0 copy-done.1
  159.4 4.4 %fusion.2 = (f32[1,512,2,256]{3,2,1,0:T(2,128)}, f32[512,2,256]{2,1,0:T(2,128)}, f32[512,2,256]{2,1,0:T(2,128)}) fusion(bf16[4,128,2,256]{3,2,1,0:T(2,128)(2,1)S(1)} %copy.17, f32[1,512,2,256]{3,2,1,0:T(2,128)S(1)} %copy-done, f32[1,512,2,256]{3,2,1,0:T(2,128)S(1)} %copy-done.1), kind=kLoop, calls=%fused_computation.6 | loop fusion | flops 3145728 | bytes 5767168 | tf_op jit(solution)/shard_map/broadcast_in_dim | solution.py:701
  (5 shorter events, 0.1 us)
Async XLA Ops:
  4.5 154.9 %copy-start = (f32[1,512,2,256]{3,2,1,0:T(2,128)S(1)}, f32[1,512,2,256]{3,2,1,0:T(2,128)}, u32[]{:S(2)}) copy-start(f32[1,512,2,256]{3,2,1,0:T(2,128)} %param.15) | copy-start | bytes 3145732
  4.5 154.9 %copy-start.1 = (f32[1,512,2,256]{3,2,1,0:T(2,128)S(1)}, f32[1,512,2,256]{3,2,1,0:T(2,128)}, u32[]{:S(2)}) copy-start(f32[1,512,2,256]{3,2,1,0:T(2,128)} %param.14) | copy-start | bytes 3145732

commit v6 on v5

--- a/solution.py
+++ b/solution.py
@@ -496,18 +496,15 @@
             chip_copy(s, 1).start()
 
     products(0)
-    products(1)
     chip_sum(0)
 
     def products_step(s, carry):
         products(s)
-        chip_sum(s - 1)
-        relay_sum(s - 2)
+        chip_sum(s)
+        relay_sum(s - 1)
         return carry
 
-    lax.fori_loop(2, sections, products_step, 0)
-    chip_sum(sections - 1)
-    relay_sum(sections - 2)
+    lax.fori_loop(1, sections, products_step, 0)
     relay_sum(sections - 1)
 
     def finish(s, carry):

time: 166 us -> 165 us (level)
  no operation moved by 1% of the time
where the time goes in v6:
time: 165 us; the launch traced here: 163 us
  Pallas kernels  153 us (93%)
  other arithmetic  5.87 us (4%)
  local copies, waits for them, and re-layouts  3.56 us (2%)
    pallas_call x1, Pallas kernels, chain(): pl.pallas_call(functools.partial(chain_kernel, sections, model_width, loa...  153 us
    broadcast_in_dim x1, other arithmetic, on_device(): direction[None]  4.41 us

profile of v6, /device:TPU:0, one launch (start us, length us, event | category | flops | bytes accessed | tf_op | source)
XLA Modules:
  0.0 162.8 jit_solution(13496709346249315192)
XLA Ops:
  0.6 0.7 broadcast_subtract_fusion
  1.3 0.1 broadcast_in_dim.17
  1.4 0.1 eq.24
  1.5 0.7 broadcast_in_dim.18
  2.2 0.1 reshape.42
  2.3 0.7 copy.14
  3.0 0.1 fusion.3
  3.2 1.3 copy.20
  4.5 0.0 copy-start
  4.5 0.0 copy-start.1
  4.5 152.7 %shard_map.111 = (bf16[4,2,128,256]{3,2,1,0:T(8,128)(2,1)S(1)}, f32[8,128]{1,0:T(8,128)S(1)}) custom-call(bf16[256,4096]{1,0:T(8,128)(2,1)} %tokens_ref.1, bf16[256,4096]{1,0:T(8,128)(2,1)} %cotangent_ref.1, f32[4,1,1024]{2,1,0:T(1,128)S(1)} %bitcast.26, f32[256,128]{1,0:T(8,128)S(1)} %pad_convert_fusion.owners_ref, ...), custom_call_target="tpu_custom_call" | custom-call | tf_op jit(solution)/shard_map/pallas_call | solution.py:600
  157.3 0.5 copy.17
  157.8 0.6 multiply_reduce_fusion
  158.4 0.0 copy-done
  158.4 0.0 copy-done.1
  158.4 4.4 %fusion.2 = (f32[1,512,2,256]{3,2,1,0:T(2,128)}, f32[512,2,256]{2,1,0:T(2,128)}, f32[512,2,256]{2,1,0:T(2,128)}) fusion(bf16[4,128,2,256]{3,2,1,0:T(2,128)(2,1)S(1)} %copy.17, f32[1,512,2,256]{3,2,1,0:T(2,128)S(1)} %copy-done, f32[1,512,2,256]{3,2,1,0:T(2,128)S(1)} %copy-done.1), kind=kLoop, calls=%fused_computation.6 | loop fusion | flops 3145728 | bytes 5767168 | tf_op jit(solution)/shard_map/broadcast_in_dim | solution.py:698
  (5 shorter events, 0.1 us)
Async XLA Ops:
  4.5 153.9 %copy-start = (f32[1,512,2,256]{3,2,1,0:T(2,128)S(1)}, f32[1,512,2,256]{3,2,1,0:T(2,128)}, u32[]{:S(2)}) copy-start(f32[1,512,2,256]{3,2,1,0:T(2,128)} %param.15) | copy-start | bytes 3145732
  4.5 153.9 %copy-start.1 = (f32[1,512,2,256]{3,2,1,0:T(2,128)S(1)}, f32[1,512,2,256]{3,2,1,0:T(2,128)}, u32[]{:S(2)}) copy-start(f32[1,512,2,256]{3,2,1,0:T(2,128)} %param.14) | copy-start | bytes 3145732

commit v7 on v6

--- a/solution.py
+++ b/solution.py
@@ -239,7 +239,6 @@
         )
 
     spread_rows(0)
-    rows_left(0)
     spread_rows(1)
 
     def copies(make, slot):
@@ -322,7 +321,7 @@
 
         @pl.when(s + 2 < sections)
         def _():
-            rows_left(s + 1)
+            rows_left(s)
             spread_rows(s + 2)
 
         for h in range(HALVES):
@@ -562,6 +561,7 @@
 
         return carry
 
+    rows_left(sections - 2)
     rows_left(sections - 1)
     lax.fori_loop(0, sections, drain_rows, 0)
 

time: 165 us -> 159 us (0.964)
  Pallas kernels: 153 us -> 147 us
    pallas_call x1, Pallas kernels: 153 us -> 147 us  [chain(): pl.pallas_call(functools.partial(chain_kernel, sections, model_width, loa...]
where the time goes in v7:
time: 159 us; the launch traced here: 157 us
  Pallas kernels  147 us (92%)
  other arithmetic  5.87 us (4%)
  local copies, waits for them, and re-layouts  3.56 us (2%)
    pallas_call x1, Pallas kernels, chain(): pl.pallas_call(functools.partial(chain_kernel, sections, model_width, loa...  147 us
    broadcast_in_dim x1, other arithmetic, on_device(): direction[None]  4.41 us

profile of v7, /device:TPU:0, one launch (start us, length us, event | category | flops | bytes accessed | tf_op | source)
XLA Modules:
  0.0 156.7 jit_solution(10381865936414381980)
XLA Ops:
  0.6 0.7 broadcast_subtract_fusion
  1.3 0.1 broadcast_in_dim.17
  1.4 0.1 eq.24
  1.5 0.7 broadcast_in_dim.18
  2.2 0.1 reshape.42
  2.3 0.7 copy.14
  3.0 0.1 fusion.3
  3.2 1.3 copy.20
  4.5 0.0 copy-start
  4.5 0.0 copy-start.1
  4.5 146.5 %shard_map.111 = (bf16[4,2,128,256]{3,2,1,0:T(8,128)(2,1)S(1)}, f32[8,128]{1,0:T(8,128)S(1)}) custom-call(bf16[256,4096]{1,0:T(8,128)(2,1)} %tokens_ref.1, bf16[256,4096]{1,0:T(8,128)(2,1)} %cotangent_ref.1, f32[4,1,1024]{2,1,0:T(1,128)S(1)} %bitcast.26, f32[256,128]{1,0:T(8,128)S(1)} %pad_convert_fusion.owners_ref, ...), custom_call_target="tpu_custom_call" | custom-call | tf_op jit(solution)/shard_map/pallas_call | solution.py:600
  151.1 0.5 copy.17
  151.6 0.6 multiply_reduce_fusion
  152.3 0.0 copy-done
  152.3 0.0 copy-done.1
  152.3 4.4 %fusion.2 = (f32[1,512,2,256]{3,2,1,0:T(2,128)}, f32[512,2,256]{2,1,0:T(2,128)}, f32[512,2,256]{2,1,0:T(2,128)}) fusion(bf16[4,128,2,256]{3,2,1,0:T(2,128)(2,1)S(1)} %copy.17, f32[1,512,2,256]{3,2,1,0:T(2,128)S(1)} %copy-done, f32[1,512,2,256]{3,2,1,0:T(2,128)S(1)} %copy-done.1), kind=kLoop, calls=%fused_computation.6 | loop fusion | flops 3145728 | bytes 5767168 | tf_op jit(solution)/shard_map/broadcast_in_dim | solution.py:698
  (5 shorter events, 0.1 us)
Async XLA Ops:
  4.5 147.7 %copy-start = (f32[1,512,2,256]{3,2,1,0:T(2,128)S(1)}, f32[1,512,2,256]{3,2,1,0:T(2,128)}, u32[]{:S(2)}) copy-start(f32[1,512,2,256]{3,2,1,0:T(2,128)} %param.15) | copy-start | bytes 3145732
  4.5 147.7 %copy-start.1 = (f32[1,512,2,256]{3,2,1,0:T(2,128)S(1)}, f32[1,512,2,256]{3,2,1,0:T(2,128)}, u32[]{:S(2)}) copy-start(f32[1,512,2,256]{3,2,1,0:T(2,128)} %param.14) | copy-start | bytes 3145732
